TPU v7x, 32 devices: a whole 2x2x4 slice. The times are simulated.
32 devices in a mesh: dp: 4 (over y, x), erow: 2 (over core), ecol: 4 (over z).
Axes of the slice: x: 2, y: 2, z: 4, core: 2. Of those that a mesh axis runs over, the one named last changes fastest.
Arguments:
- tokens: bfloat16 [16, 512, 1024], P(('dp', 'ecol'), 'erow'), may hold values from -6 to 6
- lengths: int32 [16], P(('dp', 'ecol')), may hold values from 384 to 512, as said below
- routes: int32 [16, 512, 2], P(('dp', 'ecol'), 'erow'), may hold values from 0 to 7, as said below
- attn_gain: float32 [1024], replicated, may hold values from 0.1 to 1.9
- query_weight: bfloat16 [1024, 1024], replicated, may hold values from -0.1875 to 0.1875
- key_weight: bfloat16 [1024, 1024], replicated, may hold values from -0.1875 to 0.1875
- value_weight: bfloat16 [1024, 1024], replicated, may hold values from -0.1875 to 0.1875
- out_weight: bfloat16 [1024, 1024], replicated, may hold values from -1.5 to 1.5
- relative_bias: float32 [16, 32], replicated, may hold values from -4 to 4
- moe_gain: float32 [1024], replicated, may hold values from 0.1 to 1.9
- router_weight: float32 [1024, 8], replicated, may hold values from -0.09375 to 0.09375
- gate_weight: bfloat16 [8, 1024, 2816], P(('erow', 'ecol')), may hold values from -0.1875 to 0.1875
- up_weight: bfloat16 [8, 1024, 2816], P(('erow', 'ecol')), may hold values from -0.1875 to 0.1875
- down_weight: bfloat16 [8, 2816, 1024], P(('erow', 'ecol')), may hold values from -4 to 4
- cotangent: bfloat16 [16, 512, 1024], P(('dp', 'ecol'), 'erow'), may hold values from -6 to 6
Outputs:
- output: bfloat16 [16, 512, 1024], P(('dp', 'ecol'), 'erow')
- grad_tokens: float32 [16, 512, 1024], P(('dp', 'ecol'), 'erow')
- grad_attn_gain: float32 [1024], P(('dp', 'erow', 'ecol'))
- grad_query: float32 [1024, 1024], P(('dp', 'erow', 'ecol'))
- grad_key: float32 [1024, 1024], P(('dp', 'erow', 'ecol'))
- grad_value: float32 [1024, 1024], P(('dp', 'erow', 'ecol'))
- grad_out: float32 [1024, 1024], P(('dp', 'erow', 'ecol'))
- grad_bias: float32 [512], P(('dp', 'erow', 'ecol'))
- grad_moe_gain: float32 [1024], P(('dp', 'erow', 'ecol'))
- grad_router: float32 [1024, 8], P(('dp', 'erow', 'ecol'))
- grad_gate: float32 [8, 1024, 2816], P(('erow', 'ecol'), 'dp')
- grad_up: float32 [8, 1024, 2816], P(('erow', 'ecol'), 'dp')
- grad_down: float32 [8, 2816, 1024], P(('erow', 'ecol'), 'dp')
Inputs may be any that keep to these rules, and one draw needn't show every extreme that they name: `lengths`: every item has more than 383 live positions; some item has exactly 512. The two experts of a position differ. In every draw one expert is named first at the first 80 positions of every aligned block of 256 positions (the rows of one device); padded positions carry routes too.
All inputs are finite; a program needn't handle non-finite values.
Results may differ from a plain program's by a relative error of at most 0.025.
Values may be sent and summed in bfloat16 or wider, within the bound.
A program may use at most 384 MiB of HBM per device.

v0:
```python
import jax
import jax.numpy as jnp
from jax import lax
from jax.sharding import PartitionSpec as P

epsilon = 1e-06
highest = lax.Precision.HIGHEST
thresholds = (12, 16, 23, 32, 46, 64, 91)


def rms_scale(inputs, norm_gain):
    return (
        inputs * lax.rsqrt(jnp.mean(inputs * inputs, axis=-1, keepdims=True) + epsilon) * norm_gain
    )


def bucket_of(offset):
    distance = jnp.abs(offset)
    larger = 8 + sum(((distance >= bound_at).astype(jnp.int32) for bound_at in thresholds))
    return jnp.where(offset > 0, 16, 0) + jnp.where(distance < 8, distance, larger)


def rounded_values(values):
    return values.astype(jnp.bfloat16)


def product(left_side, right_side):
    return jnp.dot(left_side, right_side, preferred_element_type=jnp.float32)


def product_back(left_side, right_side):
    return lax.dot_general(
        left_side, right_side, (((1,), (1,)), ((), ())), preferred_element_type=jnp.float32
    )


def product_left(left_side, right_side):
    return lax.dot_general(
        left_side, right_side, (((0,), (0,)), ((), ())), preferred_element_type=jnp.float32
    )


def sectioned_form(block_rows, capacity):
    return block_rows.reshape(
        lax.axis_size("erow"), lax.axis_size("ecol"), capacity, block_rows.shape[-1]
    )


def send_rows(block_rows, capacity):
    moved = lax.all_to_all(
        lax.all_to_all(
            sectioned_form(block_rows, capacity), "erow", split_axis=0, concat_axis=0, tiled=True
        ),
        "ecol",
        split_axis=1,
        concat_axis=1,
        tiled=True,
    )
    return moved.reshape(block_rows.shape)


def return_rows(block_rows, capacity):
    moved = lax.all_to_all(
        lax.all_to_all(
            sectioned_form(block_rows, capacity), "erow", split_axis=0, concat_axis=0, tiled=True
        ),
        "ecol",
        split_axis=1,
        concat_axis=1,
        tiled=True,
    )
    return moved.reshape(block_rows.shape)


def send_pairs(block_rows, block_grads, capacity):
    transferred_rows, moved_grads = (
        lax.all_to_all(
            lax.all_to_all(
                sectioned_form(block_rows, capacity),
                "erow",
                split_axis=0,
                concat_axis=0,
                tiled=True,
            ),
            "ecol",
            split_axis=1,
            concat_axis=1,
            tiled=True,
        ),
        lax.all_to_all(
            lax.all_to_all(
                sectioned_form(block_grads, capacity),
                "erow",
                split_axis=0,
                concat_axis=0,
                tiled=True,
            ),
            "ecol",
            split_axis=1,
            concat_axis=1,
            tiled=True,
        ),
    )
    return (transferred_rows.reshape(block_rows.shape), moved_grads.reshape(block_grads.shape))


def return_pairs(block_rows, block_grads, capacity):
    transferred_rows, moved_grads = (
        lax.all_to_all(
            lax.all_to_all(
                sectioned_form(block_rows, capacity),
                "erow",
                split_axis=0,
                concat_axis=0,
                tiled=True,
            ),
            "ecol",
            split_axis=1,
            concat_axis=1,
            tiled=True,
        ),
        lax.all_to_all(
            lax.all_to_all(
                sectioned_form(block_grads, capacity),
                "erow",
                split_axis=0,
                concat_axis=0,
                tiled=True,
            ),
            "ecol",
            split_axis=1,
            concat_axis=1,
            tiled=True,
        ),
    )
    return (transferred_rows.reshape(block_rows.shape), moved_grads.reshape(block_grads.shape))


def expert_hidden(received, gate_mat, up_mat):
    gate_part = product(received, gate_mat)
    up_part = product(received, up_mat)
    hidden = rounded_values(jax.nn.gelu(gate_part) * up_part)
    return (gate_part, up_part, hidden)


def part_grads(gate_part, up_part, hidden_grad):
    gelu_value, gelu_pull = jax.vjp(jax.nn.gelu, gate_part)
    gate_part_grad = rounded_values(gelu_pull(hidden_grad * up_part)[0])
    up_part_grad = rounded_values(hidden_grad * gelu_value)
    return (gate_part_grad, up_part_grad)


def body(
    tokens,
    lengths,
    routes,
    attn_gain,
    query_weight,
    key_weight,
    value_weight,
    out_weight,
    relative_bias,
    moe_gain,
    router_weight,
    gate_weight,
    up_weight,
    down_weight,
    cotangent,
):
    tok_rows = tokens.shape[1]
    model_width = tokens.shape[2]
    head_count, bucket_count = relative_bias.shape
    head_size = model_width // head_count
    expert_count = router_weight.shape[1]
    capacity = 5 * tok_rows // (2 * expert_count)
    slot_count = expert_count * capacity
    piece_index = lax.axis_index("erow")
    seq_rows = tok_rows * lax.axis_size("erow")
    inputs = tokens[0].astype(jnp.float32)
    seq_length = lengths[0]
    gate_mat = gate_weight[0]
    up_mat = up_weight[0]
    down_mat = down_weight[0]
    hidden_width = gate_mat.shape[1]
    query_pos = piece_index * tok_rows + jnp.arange(tok_rows, dtype=jnp.int32)
    key_pos = jnp.arange(seq_rows, dtype=jnp.int32)
    bucket_ids = bucket_of(key_pos[None, :] - query_pos[:, None])
    bias_onehot_table = (
        jnp.arange(bucket_count, dtype=jnp.int32)[:, None, None] == bucket_ids[None]
    ).astype(jnp.bfloat16)
    bias_full = jnp.einsum(
        "zt,tyx->zyx",
        relative_bias,
        bias_onehot_table,
        precision=highest,
        preferred_element_type=jnp.float32,
    )
    key_live = key_pos < seq_length
    tok_live = query_pos < seq_length
    pair_routes = routes[0]
    route_flat = pair_routes.reshape(-1)
    pair_live = jnp.broadcast_to(tok_live[:, None], pair_routes.shape).reshape(-1)
    expert_range = jnp.arange(expert_count, dtype=jnp.int32)
    route_hot = ((route_flat[:, None] == expert_range[None, :]) & pair_live[:, None]).astype(
        jnp.int32
    )
    earlier = jnp.cumsum(route_hot, axis=0) - route_hot
    position = jnp.sum(earlier * route_hot, axis=1)
    kept_pairs = pair_live & (position < capacity)
    slot_ids = jnp.where(kept_pairs, route_flat * capacity + position, -1).reshape(tok_rows, 2)
    slot_range = jnp.arange(slot_count, dtype=jnp.int32)
    select_lead = (slot_ids[:, 0:1] == slot_range[None, :]).astype(jnp.bfloat16)
    select_trail = (slot_ids[:, 1:2] == slot_range[None, :]).astype(jnp.bfloat16)
    select_both = select_lead + select_trail
    choice_hot = (pair_routes[:, :, None] == expert_range[None, None, :]).astype(jnp.float32)

    def front():
        normalized_reduced = rounded_values(rms_scale(inputs, attn_gain))
        queries = rounded_values(product(normalized_reduced, query_weight))
        keys_local = rounded_values(product(normalized_reduced, key_weight))
        values_local = rounded_values(product(normalized_reduced, value_weight))
        gathered_keys, values_all = (
            lax.all_gather(keys_local, "erow", axis=0, tiled=True),
            lax.all_gather(values_local, "erow", axis=0, tiled=True),
        )
        query_heads = queries.reshape(tok_rows, head_count, head_size)
        key_heads = gathered_keys.reshape(seq_rows, head_count, head_size)
        value_heads = values_all.reshape(seq_rows, head_count, head_size)
        scores = (
            jnp.einsum("qhd,khd->hqk", query_heads, key_heads, preferred_element_type=jnp.float32)
            * 0.125
            + bias_full
        )
        scores = jnp.where(key_live[None, None, :], scores, -1000000000.0)
        attn_probs = jax.nn.softmax(scores, axis=-1)
        probs_low = rounded_values(attn_probs)
        mixed = rounded_values(
            jnp.einsum(
                "hqk,khd->qhd", probs_low, value_heads, preferred_element_type=jnp.float32
            ).reshape(tok_rows, model_width)
        )
        residual = inputs + product(mixed, out_weight)
        moe_in = rms_scale(residual, moe_gain)
        logits = jnp.dot(moe_in, router_weight, precision=highest)
        gate_probs = jax.nn.softmax(logits, axis=-1)
        gate_pick = jnp.sum(gate_probs[:, None, :] * choice_hot, axis=-1)
        rows_buffer = rounded_values(
            jnp.einsum(
                "ts,td->sd", select_both, rounded_values(moe_in), preferred_element_type=jnp.float32
            )
        )
        return (
            normalized_reduced,
            query_heads,
            key_heads,
            value_heads,
            attn_probs,
            probs_low,
            mixed,
            residual,
            moe_in,
            gate_probs,
            gate_pick,
            rows_buffer,
        )

    first_pass = front()
    received = send_rows(first_pass[11], capacity)
    first_hidden = expert_hidden(received, gate_mat, up_mat)[2]
    expert_out = rounded_values(product(first_hidden, down_mat))
    returned = return_rows(expert_out, capacity)
    pair_lead = product(select_lead, returned)
    pair_trail = product(select_trail, returned)
    gate_pick = first_pass[10]
    output = rounded_values(
        first_pass[7] + gate_pick[:, 0:1] * pair_lead + gate_pick[:, 1:2] * pair_trail
    )
    (
        normalized_reduced,
        query_heads,
        key_heads,
        value_heads,
        attn_probs,
        probs_low,
        mixed,
        residual,
        moe_in,
        gate_probs,
        gate_pick,
        rows_buffer,
    ) = front()
    out_grad = cotangent[0].astype(jnp.float32)
    grad_buffer = rounded_values(
        jnp.einsum(
            "ts,td->sd",
            select_lead,
            rounded_values(gate_pick[:, 0:1] * out_grad),
            preferred_element_type=jnp.float32,
        )
        + jnp.einsum(
            "ts,td->sd",
            select_trail,
            rounded_values(gate_pick[:, 1:2] * out_grad),
            preferred_element_type=jnp.float32,
        )
    )
    received, received_grad = send_pairs(rows_buffer, grad_buffer, capacity)
    gate_part, up_part, hidden = expert_hidden(received, gate_mat, up_mat)
    expert_out = rounded_values(product(hidden, down_mat))
    hidden_grad = product_back(received_grad, down_mat)
    gate_part_grad, up_part_grad = part_grads(gate_part, up_part, hidden_grad)
    row_grad = rounded_values(
        product_back(gate_part_grad, gate_mat) + product_back(up_part_grad, up_mat)
    )
    returned, returned_grad = return_pairs(expert_out, row_grad, capacity)
    pair_lead = product(select_lead, returned)
    pair_trail = product(select_trail, returned)
    pick_grad = jnp.stack(
        [jnp.sum(out_grad * pair_lead, axis=-1), jnp.sum(out_grad * pair_trail, axis=-1)], axis=1
    )
    prob_grad = jnp.sum(pick_grad[:, :, None] * choice_hot, axis=1)
    logit_grad = gate_probs * (prob_grad - jnp.sum(gate_probs * prob_grad, axis=-1, keepdims=True))
    router_wgrad = lax.dot_general(moe_in, logit_grad, (((0,), (0,)), ((), ())), precision=highest)
    moe_in_grad = product(select_both, returned_grad) + lax.dot_general(
        logit_grad, router_weight, (((1,), (1,)), ((), ())), precision=highest
    )
    unused_moe, moe_pull = jax.vjp(rms_scale, residual, moe_gain)
    residual_part, moe_gain_grad = moe_pull(moe_in_grad)
    residual_grad = out_grad + residual_part
    branch_grad = rounded_values(residual_grad)
    out_wgrad = product_left(mixed, branch_grad)
    mixed_grad = rounded_values(product_back(branch_grad, out_weight)).reshape(
        tok_rows, head_count, head_size
    )
    prob_part = jnp.einsum(
        "qhd,khd->hqk", mixed_grad, value_heads, preferred_element_type=jnp.float32
    )
    attention_score_gradient = rounded_values(
        attn_probs * (prob_part - jnp.sum(attn_probs * prob_part, axis=-1, keepdims=True))
    )
    query_grad = rounded_values(
        jnp.einsum(
            "hqk,khd->qhd", attention_score_gradient, key_heads, preferred_element_type=jnp.float32
        )
        * 0.125
    ).reshape(tok_rows, model_width)
    key_part = (
        jnp.einsum(
            "hqk,qhd->khd",
            attention_score_gradient,
            query_heads,
            preferred_element_type=jnp.float32,
        )
        * 0.125
    ).reshape(seq_rows, model_width)
    value_part = jnp.einsum(
        "hqk,qhd->khd", probs_low, mixed_grad, preferred_element_type=jnp.float32
    ).reshape(seq_rows, model_width)
    key_sum, value_sum = (
        lax.psum_scatter(
            key_part.astype(jnp.bfloat16), "erow", scatter_dimension=0, tiled=True
        ).astype(jnp.float32),
        lax.psum_scatter(
            value_part.astype(jnp.bfloat16), "erow", scatter_dimension=0, tiled=True
        ).astype(jnp.float32),
    )
    key_grad = rounded_values(key_sum)
    value_grad = rounded_values(value_sum)
    position_bias_gradient = jnp.einsum(
        "tlx,mlx->tm",
        attention_score_gradient,
        bias_onehot_table,
        preferred_element_type=jnp.float32,
    )
    query_wgrad = product_left(normalized_reduced, query_grad)
    key_wgrad = product_left(normalized_reduced, key_grad)
    value_wgrad = product_left(normalized_reduced, value_grad)
    normed_grad = (
        product_back(query_grad, query_weight)
        + product_back(key_grad, key_weight)
        + product_back(value_grad, value_weight)
    )
    discarded_attention, attn_pull = jax.vjp(rms_scale, inputs, attn_gain)
    input_part, attn_gain_grad = attn_pull(normed_grad)
    token_grad = residual_grad + input_part
    replica_index = lax.axis_index("dp")
    width_share = model_width // lax.axis_size("dp")
    hidden_share = hidden_width // lax.axis_size("dp")
    rows_piece = lax.all_gather(received, "dp", axis=0, tiled=True)
    grads_piece = lax.all_gather(received_grad, "dp", axis=0, tiled=True)
    piece_gate, piece_up, piece_hidden = expert_hidden(rows_piece, gate_mat, up_mat)
    piece_gate_grad, piece_up_grad = part_grads(
        piece_gate, piece_up, product_back(grads_piece, down_mat)
    )
    rows_part = lax.dynamic_slice_in_dim(rows_piece, replica_index * width_share, width_share, 1)
    hidden_part = lax.dynamic_slice_in_dim(
        piece_hidden, replica_index * hidden_share, hidden_share, 1
    )
    gate_total = product_left(rows_part, piece_gate_grad)
    up_total = product_left(rows_part, piece_up_grad)
    down_total = product_left(hidden_part, grads_piece)
    gate_sum = gate_total[None]
    up_sum = up_total[None]
    down_sum = down_total[None]
    dense_sums = (
        lax.psum_scatter(attn_gain_grad, ("dp", "erow", "ecol"), scatter_dimension=0, tiled=True),
        lax.psum_scatter(query_wgrad, ("dp", "erow", "ecol"), scatter_dimension=0, tiled=True),
        lax.psum_scatter(key_wgrad, ("dp", "erow", "ecol"), scatter_dimension=0, tiled=True),
        lax.psum_scatter(value_wgrad, ("dp", "erow", "ecol"), scatter_dimension=0, tiled=True),
        lax.psum_scatter(out_wgrad, ("dp", "erow", "ecol"), scatter_dimension=0, tiled=True),
        lax.psum_scatter(
            position_bias_gradient.reshape(-1),
            ("dp", "erow", "ecol"),
            scatter_dimension=0,
            tiled=True,
        ),
        lax.psum_scatter(moe_gain_grad, ("dp", "erow", "ecol"), scatter_dimension=0, tiled=True),
        lax.psum_scatter(router_wgrad, ("dp", "erow", "ecol"), scatter_dimension=0, tiled=True),
    )
    return (
        output[None],
        token_grad[None],
        dense_sums[0],
        dense_sums[1],
        dense_sums[2],
        dense_sums[3],
        dense_sums[4],
        dense_sums[5],
        dense_sums[6],
        dense_sums[7],
        gate_sum,
        up_sum,
        down_sum,
    )


def solution(mesh):
    placed = (
        P(("dp", "ecol"), "erow", None),
        P(("dp", "ecol")),
        P(("dp", "ecol"), "erow", None),
        P(),
        P(),
        P(),
        P(),
        P(),
        P(),
        P(),
        P(),
        P(("erow", "ecol"), None, None),
        P(("erow", "ecol"), None, None),
        P(("erow", "ecol"), None, None),
        P(("dp", "ecol"), "erow", None),
    )
    return jax.shard_map(
        body,
        mesh=mesh,
        in_specs=placed,
        out_specs=(
            P(("dp", "ecol"), "erow", None),
            P(("dp", "ecol"), "erow", None),
            P(("dp", "erow", "ecol")),
            P(("dp", "erow", "ecol"), None),
            P(("dp", "erow", "ecol"), None),
            P(("dp", "erow", "ecol"), None),
            P(("dp", "erow", "ecol"), None),
            P(("dp", "erow", "ecol")),
            P(("dp", "erow", "ecol")),
            P(("dp", "erow", "ecol"), None),
            P(("erow", "ecol"), "dp", None),
            P(("erow", "ecol"), "dp", None),
            P(("erow", "ecol"), "dp", None),
        ),
        check_vma=False,
    )
```

profile of v0, /device:TPU:0, one launch (start us, length us, event | category | flops | bytes accessed | tf_op | source)
XLA Modules:
  0.0 1168.6 jit_solution(397807151605346778)
XLA Ops:
  24.4 7.3 fusion.9
  33.4 9.7 fusion.13
  52.4 14.1 %fusion.71 = bf16[16,64,256]{2,1,0:T(8,128)(2,1)} fusion(bf16[512,16,64]{0,2,1:T(8,128)(2,1)S(1)} %bitcast.203, f32[16,256]{1,0:T(8,128)S(1)} %get-tuple-element.30, f32[16,256,512]{2,1,0:T(8,128)} %copy-done.2), kind=kOutput, calls=%fused_computation.91 | convolution fusion | flops 274993664 | bytes 9977856 | tf_op jit(solution)/shard_map/hqk,khd->qhd/dot_general | solution.py:238
  69.8 4.8 all_to_all.44
  74.7 38.1 %all_to_all.45 = bf16[2,4,80,1024]{3,2,0,1:T(8,128)(2,1)S(1)} all-to-all(bf16[2,4,80,1024]{3,2,0,1:T(8,128)(2,1)S(1)} %copy.123), channel_id=1, replica_groups=mesh['dp'=4,'erow'=2,'ecol'=4] {'ecol'}, dimensions={1} | all-to-all | bytes 2621440 | tf_op jit(solution)/shard_map/all_to_all | solution.py:50
  114.0 7.1 fusion.40
  121.1 9.1 fusion.34
  135.0 4.8 all_to_all.46
  146.4 30.8 %all-to-all-done.3 = bf16[2,4,80,1024]{3,2,0,1:T(8,128)(2,1)} async-done(((bf16[2,4,80,1024]{3,2,0,1:T(8,128)(2,1)}), bf16[2,4,80,1024]{3,2,0,1:T(8,128)(2,1)}, u32[]{:S(2)}, u32[]{:S(2)}) %all-to-all-start.3) | async-done | bytes 1310752 | tf_op jit(solution)/shard_map/all_to_all | solution.py:63
  183.8 4.8 all_to_all.47
  188.7 34.5 %all_to_all.48 = bf16[2,4,80,1024]{3,2,0,1:T(8,128)(2,1)S(1)} all-to-all(bf16[2,4,80,1024]{3,2,0,1:T(8,128)(2,1)S(1)} %copy.127), channel_id=1, replica_groups=mesh['dp'=4,'erow'=2,'ecol'=4] {'ecol'}, dimensions={1} | all-to-all | bytes 2621440 | tf_op jit(solution)/shard_map/all_to_all | solution.py:90
  224.4 7.1 fusion.26
  234.5 11.0 fusion.32
  245.4 12.0 %add_convert_fusion = bf16[640,1024]{1,0:T(8,128)(2,1)S(1)} fusion(f32[640,1024]{1,0:T(8,128)} %fusion.32, bf16[1,1024,2816]{2,1,0:T(8,128)(2,1)S(1)} %bitcast.215, f32[640,2816]{1,0:T(8,128)} %copy-done.27, f32[640,2816]{1,0:T(8,128)} %copy-done.29, f32[640,2816]{1,0:T(8,128)} %copy-done.28), kind=kOutput, calls=%fused_computation.61 | convolution fusion | flops 3730145280 | bytes 31326208 | tf_op jit(solution)/shard_map/dot_general | solution.py:32
  257.5 4.8 all_to_all.49
  270.8 30.3 %all-to-all-done.7 = bf16[2,4,80,1024]{3,2,0,1:T(8,128)(2,1)} async-done(((bf16[2,4,80,1024]{3,2,0,1:T(8,128)(2,1)}), bf16[2,4,80,1024]{3,2,0,1:T(8,128)(2,1)}, u32[]{:S(2)}, u32[]{:S(2)}) %all-to-all-start.7) | async-done | bytes 1310752 | tf_op jit(solution)/shard_map/all_to_all | solution.py:122
  308.8 14.5 %fusion.64 = bf16[16,64,512]{2,1,0:T(8,128)(2,1)} fusion(bf16[256,16,64]{0,2,1:T(8,128)(2,1)} %bitcast.206, f32[16,256]{1,0:T(8,128)S(1)} %get-tuple-element.30, f32[16,256,512]{2,1,0:T(8,128)} %copy-done.2), kind=kOutput, calls=%fused_computation.79 | convolution fusion | flops 275255808 | bytes 9977856 | tf_op jit(solution)/shard_map/hqk,qhd->khd/dot_general | solution.py:356
  324.3 5.7 multiply_reduce_fusion
  349.6 64.0 %reduce-scatter.22.cloned.1.call-done = f32[32,8]{1,0:T(8,128)} async-done(((f32[1024,8]{1,0:T(8,128)}), f32[32,8]{1,0:T(8,128)}) %reduce-scatter.22.cloned.1.call-update) | async-done | bytes 1040
  415.0 6.5 fusion.79
  428.9 57.7 %all-gather.9.cloned.1.call-done = bf16[2560,1024]{1,0:T(8,128)(2,1)} async-done(((bf16[640,1024]{1,0:T(8,128)(2,1)}), bf16[2560,1024]{1,0:T(8,128)(2,1)}) %all-gather.9.cloned.1.call-update) | async-done | bytes 5242896 | tf_op jit(solution)/shard_map/all_gather | solution.py:389
  486.6 22.7 %fusion.30 = f32[2560,2816]{1,0:T(8,128)} fusion(bf16[2560,1024]{1,0:T(8,128)(2,1)} %all-gather.9.cloned.1.call-done, bf16[1,1024,2816]{2,1,0:T(8,128)(2,1)} %param.27), kind=kOutput, calls=%fused_computation.44 | convolution fusion | flops 14763950080 | bytes 39845888 | tf_op jit(solution)/shard_map/dot_general | solution.py:28
  509.3 29.8 %multiply_multiply_fusion.2 = (f32[2560,2816]{1,0:T(8,128)}, f32[2560,2816]{1,0:T(8,128)}) fusion(bf16[2560,1024]{1,0:T(8,128)(2,1)} %all-gather.9.cloned.1.call-done, bf16[1,1024,2816]{2,1,0:T(8,128)(2,1)} %param.26), kind=kOutput, calls=%fused_computation.11 | convolution fusion | flops 14821621760 | bytes 68681728 | tf_op jit(solution)/shard_map/dot_general | solution.py:28
  543.8 40.2 %all-reduce.3 = (f32[1024]{0:T(1024)S(1)}, f32[512]{0:T(512)S(1)}, f32[1024]{0:T(1024)S(1)}) all-reduce(f32[1024]{0:T(1024)S(1)} %get-tuple-element.15, f32[512]{0:T(512)S(1)} %reshape.249, f32[1024]{0:T(1024)S(1)} %get-tuple-element.13), channel_id=4, replica_groups=mesh['dp'=4,'erow'=2,'ecol'=4] {'dp','erow','ecol'}, use_global_device_ids=true, to_apply=%region_20.21.clone | all-reduce | flops 2560 | bytes 20480
  592.5 22.6 %fusion.24 = f32[2560,2816]{1,0:T(8,128)} fusion(bf16[2560,1024]{1,0:T(8,128)(2,1)} %all-gather.11.cloned.1.call-done, bf16[1,2816,1024]{2,1,0:T(8,128)(2,1)} %param.28), kind=kOutput, calls=%fused_computation.38 | convolution fusion | flops 14763950080 | bytes 39845888 | tf_op jit(solution)/shard_map/dot_general | solution.py:32
  615.1 24.0 %fusion.43 = f32[1,256,2816]{2,1,0:T(8,128)} fusion(f32[2560,2816]{1,0:T(8,128)} %fusion.24, bf16[2560,1024]{1,0:T(8,128)(2,1)} %all-gather.9.cloned.1.call-done, s32[]{:T(128)S(6)} %select_n.36, f32[2560,2816]{1,0:T(8,128)} %get-tuple-element.42), kind=kOutput, calls=%fused_computation.58 | convolution fusion | flops 3763077120 | bytes 61865988 | tf_op jit(solution)/shard_map/dot_general | solution.py:38
  639.1 13.5 %fusion.54 = f32[1,704,1024]{2,1,0:T(8,128)} fusion(bf16[2560,1024]{1,0:T(8,128)(2,1)S(1)} %bitcast.219, f32[2560,2816]{1,0:T(8,128)} %fusion.30, s32[]{:T(128)S(6)} %select_n.37, f32[2560,2816]{1,0:T(8,128)} %get-tuple-element.41), kind=kOutput, calls=%fused_computation.73 | convolution fusion | flops 3694592000 | bytes 23855108 | tf_op jit(solution)/shard_map/dot_general | solution.py:38
  652.6 34.4 %fusion.44 = f32[1,256,2816]{2,1,0:T(8,128)} fusion(f32[2560,2816]{1,0:T(8,128)} %get-tuple-element.42, f32[2560,2816]{1,0:T(8,128)} %fusion.24, f32[2560,2816]{1,0:T(8,128)} %fusion.30, bf16[2560,1024]{1,0:T(8,128)(2,1)} %all-gather.9.cloned.1.call-done, s32[]{:T(128)S(6)} %select_n.36), kind=kOutput, calls=%fused_computation.59 | convolution fusion | flops 3842375680 | bytes 90701824 | tf_op jit(solution)/shard_map/dot_general | solution.py:38
  687.0 27.0 %reduce-scatter.20.cloned.1.call-done = f32[32,1024]{1,0:T(8,128)} async-done(((f32[1024,1024]{1,0:T(8,128)}), f32[32,1024]{1,0:T(8,128)}) %reduce-scatter.20.cloned.1.call-update) | async-done | bytes 131088 | tf_op jit(solution)/shard_map/reduce_scatter | solution.py:410
  714.0 149.4 %reduce-scatter.14.cloned.1.call-done = f32[32,1024]{1,0:T(8,128)} async-done(((f32[1024,1024]{1,0:T(8,128)}), f32[32,1024]{1,0:T(8,128)}) %reduce-scatter.14.cloned.1.call-update) | async-done | bytes 131088 | tf_op jit(solution)/shard_map/reduce_scatter | solution.py:407
  863.3 149.4 %reduce-scatter.18.cloned.1.call-done = f32[32,1024]{1,0:T(8,128)} async-done(((f32[1024,1024]{1,0:T(8,128)}), f32[32,1024]{1,0:T(8,128)}) %reduce-scatter.18.cloned.1.call-update) | async-done | bytes 131088 | tf_op jit(solution)/shard_map/reduce_scatter | solution.py:409
  1012.8 148.8 %reduce-scatter.16.cloned.1.call-done = f32[32,1024]{1,0:T(8,128)} async-done(((f32[1024,1024]{1,0:T(8,128)}), f32[32,1024]{1,0:T(8,128)}) %reduce-scatter.16.cloned.1.call-update) | async-done | bytes 131088 | tf_op jit(solution)/shard_map/reduce_scatter | solution.py:408
  (182 shorter events, 112.6 us)
Async XLA Ops:
  7.2 11.8 %copy-start.3 = (bf16[1,256,1024]{2,1,0:T(8,128)(2,1)S(1)}, bf16[1,256,1024]{2,1,0:T(8,128)(2,1)}, u32[]{:S(2)}) copy-start(bf16[1,256,1024]{2,1,0:T(8,128)(2,1)} %param.15) | copy-start | bytes 1572868
  7.2 11.8 %copy-start.22 = (f32[1024]{0:T(1024)S(1)}, f32[1024]{0:T(1024)}, u32[]{:S(2)}) copy-start(f32[1024]{0:T(1024)} %param.18) | copy-start | bytes 12292
  7.2 24.5 %all-gather.7.cloned.1.call-start = ((), (), s32[]{:S(2)}) async-start(), calls=%async_computation.16 | async-start | bytes 1572864 | tf_op jit(solution)/shard_map/all_gather | solution.py:223
  8.6 15.8 %copy-start.23 = (f32[256]{0:T(256)}, f32[256]{0:T(256)S(1)}, u32[]{:S(2)}) copy-start(f32[256]{0:T(256)S(1)} %fusion.84) | copy-start | bytes 3076
  8.7 15.7 %copy-start.25 = (f32[16,32]{1,0:T(8,128)S(1)}, f32[16,32]{1,0:T(8,128)}, u32[]{:S(2)}) copy-start(f32[16,32]{1,0:T(8,128)} %param.23) | copy-start | bytes 6148
  12.0 38.8 %all-gather.5.cloned.1.call-start = ((), (), s32[]{:S(2)}) async-start(), calls=%async_computation.15 | async-start | bytes 1572864 | tf_op jit(solution)/shard_map/all_gather | solution.py:224
  19.0 12.7 %copy-start.13 = (s32[256,512]{1,0:T(8,128)}, s32[256,512]{1,0:T(8,128)S(1)}, u32[]{:S(2)}) copy-start(s32[256,512]{1,0:T(8,128)S(1)} %fusion.109) | copy-start | bytes 1572868
  33.4 9.7 copy-start.8
  52.3 14.1 %copy-start.18 = (bf16[512,1024]{0,1:T(8,128)(2,1)}, bf16[512,1024]{0,1:T(8,128)(2,1)S(1)}, u32[]{:S(2)}) copy-start(bf16[512,1024]{0,1:T(8,128)(2,1)S(1)} %copy.115) | copy-start | bytes 3145732
  52.4 16.8 %copy-start.21 = (f32[1024]{0:T(1024)S(1)}, f32[1024]{0:T(1024)}, u32[]{:S(2)}) copy-start(f32[1024]{0:T(1024)} %param.24) | copy-start | bytes 12292
  114.0 16.3 %slice-start.2 = ((s8[5767168]{0:T(1024)(128)(4,1)}), s8[4194304]{0:T(1024)(128)(4,1)S(1)}, s32[]{:S(2)}) async-start(s8[5767168]{0:T(1024)(128)(4,1)} %bitcast.216), calls=%async_computation.28 | async-start | bytes 8388608
  121.1 9.2 copy-start.27
  121.1 9.2 slice-start.3
  135.0 10.3 copy-start.20
  140.9 36.3 %all-to-all-start.3 = ((bf16[2,4,80,1024]{3,2,0,1:T(8,128)(2,1)}), bf16[2,4,80,1024]{3,2,0,1:T(8,128)(2,1)}, u32[]{:S(2)}, u32[]{:S(2)}) async-start(bf16[2,4,80,1024]{3,2,0,1:T(8,128)(2,1)} %copy.125), calls=%async_computation.3 | async-start | bytes 2621440 | tf_op jit(solution)/shard_map/all_to_all | solution.py:63
  224.4 21.1 %slice-start = ((s8[5767168]{0:T(1024)(128)(4,1)}), s8[4194304]{0:T(1024)(128)(4,1)S(1)}, s32[]{:S(2)}) async-start(s8[5767168]{0:T(1024)(128)(4,1)} %bitcast.214), calls=%async_computation.26 | async-start | bytes 8388608
  234.5 11.0 slice-start.1
  263.4 37.6 %all-to-all-start.7 = ((bf16[2,4,80,1024]{3,2,0,1:T(8,128)(2,1)}), bf16[2,4,80,1024]{3,2,0,1:T(8,128)(2,1)}, u32[]{:S(2)}, u32[]{:S(2)}) async-start(bf16[2,4,80,1024]{3,2,0,1:T(8,128)(2,1)} %copy.129), calls=%async_computation.7 | async-start | bytes 2621440 | tf_op jit(solution)/shard_map/all_to_all | solution.py:122
  267.7 145.9 %reduce-scatter.22.cloned.1.call-start = ((), (), s32[]{:S(2)}) async-start(), calls=%async_computation.25 | async-start | bytes 540672
  270.7 154.1 %reduce-scatter.12.cloned.1.call-start = ((), (), s32[]{:S(2)}) async-start(), calls=%async_computation.18 | async-start | bytes 1572864 | tf_op jit(solution)/shard_map/reduce_scatter | solution.py:363
  308.8 15.5 %copy-start.19 = (bf16[512,1024]{0,1:T(8,128)(2,1)S(1)}, bf16[512,1024]{0,1:T(8,128)(2,1)}, u32[]{:S(2)}) copy-start(bf16[512,1024]{0,1:T(8,128)(2,1)} %copy-done.18) | copy-start | bytes 3145732
  323.2 163.4 %all-gather.9.cloned.1.call-start = ((), (), s32[]{:S(2)}) async-start(), calls=%async_computation.23 | async-start | bytes 6553600 | tf_op jit(solution)/shard_map/all_gather | solution.py:389
  323.8 215.3 %reduce-scatter.10.cloned.1.call-start = ((), (), s32[]{:S(2)}) async-start(), calls=%async_computation.17 | async-start | bytes 1572864 | tf_op jit(solution)/shard_map/reduce_scatter | solution.py:360
  338.0 254.4 %all-gather.11.cloned.1.call-start = ((), (), s32[]{:S(2)}) async-start(), calls=%async_computation.24 | async-start | bytes 6553600 | tf_op jit(solution)/shard_map/all_gather | solution.py:390
  338.8 375.2 %reduce-scatter.20.cloned.1.call-start = ((), (), s32[]{:S(2)}) async-start(), calls=%async_computation.22 | async-start | bytes 4325376 | tf_op jit(solution)/shard_map/reduce_scatter | solution.py:410
  342.8 520.6 %reduce-scatter.14.cloned.1.call-start = ((), (), s32[]{:S(2)}) async-start(), calls=%async_computation.19 | async-start | bytes 4325376 | tf_op jit(solution)/shard_map/reduce_scatter | solution.py:407
  349.5 663.2 %reduce-scatter.18.cloned.1.call-start = ((), (), s32[]{:S(2)}) async-start(), calls=%async_computation.21 | async-start | bytes 4325376 | tf_op jit(solution)/shard_map/reduce_scatter | solution.py:409
  428.7 732.9 %reduce-scatter.16.cloned.1.call-start = ((), (), s32[]{:S(2)}) async-start(), calls=%async_computation.20 | async-start | bytes 4325376 | tf_op jit(solution)/shard_map/reduce_scatter | solution.py:408
  509.3 32.6 %copy-start.16 = (bf16[256,1024]{0,1:T(8,128)(2,1)S(1)}, bf16[256,1024]{0,1:T(8,128)(2,1)}, u32[]{:S(2)}) copy-start(bf16[256,1024]{0,1:T(8,128)(2,1)} %reduce-scatter.12.cloned.1.call-done) | copy-start | bytes 1572868
  539.1 46.6 %copy-start.24 = (f32[256]{0:T(256)S(1)}, f32[256]{0:T(256)}, u32[]{:S(2)}) copy-start(f32[256]{0:T(256)} %copy-done.23) | copy-start | bytes 3076
  592.5 46.6 %slice-start.4 = ((s8[5242880]{0:T(1024)(128)(4,1)}), s8[4194304]{0:T(1024)(128)(4,1)S(1)}, s32[]{:S(2)}) async-start(s8[5242880]{0:T(1024)(128)(4,1)} %bitcast.218), calls=%async_computation.30 | async-start | bytes 8388608
  615.1 24.0 %slice-start.5 = ((s8[5242880]{0:T(1024)(128)(4,1)}), s8[1048576]{0:T(1024)(128)(4,1)S(1)}, s32[]{:S(2)}) async-start(s8[5242880]{0:T(1024)(128)(4,1)} %bitcast.218), calls=%async_computation.31 | async-start | bytes 2097152
  (17 other events, 75.4 us)
Sparse Core Ops, SparseCore 0:
  12.2 11.7 all-gather.6
  26.1 10.2 all-gather.4
  270.8 142.7 reduce-scatter.21
  415.8 5.8 reduce-scatter.11
  424.0 62.5 all-gather.8
  488.7 8.5 reduce-scatter.9
  499.8 63.2 all-gather.10
  566.1 147.7 reduce-scatter.19
  716.9 146.3 reduce-scatter.13
  866.1 146.5 reduce-scatter.17
  1015.7 145.8 reduce-scatter.15
where the time goes:
time: 1170 us
  waiting for transfers between devices  659 us (56%)
  matrix products  308 us (26%)
  blocking collectives  132 us (11%)
  local copies, waits for them, and re-layouts  28.1 us (2%)
  other arithmetic  16.4 us (1%)
  between operations  15.6 us (1%)
    reduce_scatter x1, waiting for transfers between devices, body(): lax.psum_scatter(value_wgrad, ('dp', 'erow', 'ecol'), scatter_dimension=0...  149 us
    reduce_scatter x1, waiting for transfers between devices, body(): lax.psum_scatter(query_wgrad, ('dp', 'erow', 'ecol'), scatter_dimension=0...  149 us
    reduce_scatter x1, waiting for transfers between devices, body(): lax.psum_scatter(key_wgrad, ('dp', 'erow', 'ecol'), scatter_dimension=0,...  149 us
    dot_general x12, matrix products, product(): return jnp.dot(left_side, right_side, preferred_element_type=jnp.float32)  89.7 us
    dot_general x7, matrix products, product_left(): lax.dot_general(left_side, right_side, (((0,), (0,)), ((), ())), preferre...  86.3 us
    unnamed x12, waiting for transfers between devices  65.4 us
    dot_general x8, matrix products, product_back(): lax.dot_general(left_side, right_side, (((1,), (1,)), ((), ())), preferre...  61.4 us
    all_gather x1, waiting for transfers between devices, body(): rows_piece = lax.all_gather(received, 'dp', axis=0, tiled=True)  57.7 us
  transfers between devices with their start and end apart: 13, of which 8 were waited for; matrix products, arithmetic and copies ran while one was open for 22% of the time, Pallas kernels for 0%

commit v1 on v0

v1 whole, which is shorter than its diff:
```python
import functools

import jax
import jax.numpy as jnp
from jax import lax
from jax.experimental import pallas as pl
from jax.experimental.pallas import tpu as pltpu
from jax.sharding import PartitionSpec as P

epsilon = 1e-06
highest = lax.Precision.HIGHEST
thresholds = (12, 16, 23, 32, 46, 64, 91)
MESH = pl.DeviceIdType.MESH
LANES = 128
VMEM_LIMIT = 60 * 1024 * 1024


def rms_scale(inputs, norm_gain):
    return (
        inputs * lax.rsqrt(jnp.mean(inputs * inputs, axis=-1, keepdims=True) + epsilon) * norm_gain
    )


def bucket_of(offset):
    distance = jnp.abs(offset)
    larger = 8 + sum(((distance >= bound_at).astype(jnp.int32) for bound_at in thresholds))
    return jnp.where(offset > 0, 16, 0) + jnp.where(distance < 8, distance, larger)


def rounded(values):
    return values.astype(jnp.bfloat16)


def product(left_side, right_side):
    return jnp.dot(left_side, right_side, preferred_element_type=jnp.float32)


def product_back(left_side, right_side):
    return lax.dot_general(
        left_side, right_side, (((1,), (1,)), ((), ())), preferred_element_type=jnp.float32
    )


def product_left(left_side, right_side):
    return lax.dot_general(
        left_side, right_side, (((0,), (0,)), ((), ())), preferred_element_type=jnp.float32
    )


def greet(devices):
    barrier = pltpu.get_barrier_semaphore()
    for device in devices:
        pl.semaphore_signal(barrier, 1, device_id=device, device_id_type=MESH)
    pl.semaphore_wait(barrier, len(devices))


def remote(source, target, send_sem, recv_sem, device):
    return pltpu.make_async_remote_copy(
        src_ref=source,
        dst_ref=target,
        send_sem=send_sem,
        recv_sem=recv_sem,
        device_id=device,
        device_id_type=MESH,
    )


def exchange_kernel(sizes, blocks, landed, send_sems, recv_sems, own_sem):
    rows, columns = sizes
    group = rows * columns
    me = lax.axis_index("erow") * columns + lax.axis_index("ecol")
    peers = []
    for shift in range(1, group):
        peer = lax.rem(me + shift, group)
        peers.append((peer, {"erow": lax.div(peer, columns), "ecol": lax.rem(peer, columns)}))
    greet([device for _, device in peers])
    own = pltpu.make_async_copy(blocks.at[me], landed.at[me], own_sem)
    own.start()
    copies = []
    for at, (peer, device) in enumerate(peers):
        copy = remote(blocks.at[peer], landed.at[me], send_sems.at[at], recv_sems.at[at], device)
        copy.start()
        copies.append(copy)
    for copy in copies:
        copy.wait()
    own.wait()


def exchange(blocks, sizes, number):
    peers = sizes[0] * sizes[1] - 1
    return pl.pallas_call(
        functools.partial(exchange_kernel, sizes),
        out_shape=jax.ShapeDtypeStruct(blocks.shape, blocks.dtype),
        in_specs=[pl.BlockSpec(memory_space=pl.ANY)],
        out_specs=pl.BlockSpec(memory_space=pl.ANY),
        scratch_shapes=[
            pltpu.SemaphoreType.DMA((peers,)),
            pltpu.SemaphoreType.DMA((peers,)),
            pltpu.SemaphoreType.DMA,
        ],
        compiler_params=pltpu.CompilerParams(collective_id=number, has_side_effects=True),
    )(blocks)


def replicas(block):
    half = block.shape[0] // 2
    first = [(at, at ^ 1) for at in range(4)]
    second = [(at, at ^ 2) for at in range(4)]
    by_first = lax.ppermute(block, "dp", first)
    by_second = lax.ppermute(block, "dp", second)
    upper = lax.ppermute(by_first[:half], "dp", second)
    lower = lax.ppermute(by_second[half:], "dp", first)
    return jnp.concatenate([block, by_first, by_second, upper, lower], axis=0)


def reduce_kernel(sizes, widths, *refs):
    n_dp, n_row, n_col, depth = sizes
    count = len(widths)
    grads, totals = refs[:count], refs[count : 2 * count]
    held = [refs[2 * count + 7 * at : 2 * count + 7 * at + 7] for at in range(count)]
    send_sems, recv_sems = refs[-2:]
    dp, row, col = lax.axis_index("dp"), lax.axis_index("erow"), lax.axis_index("ecol")
    slow, fast = lax.div(dp, 2), lax.rem(dp, 2)
    over_row = {"erow": 1 - row}
    over_fast = {"dp": slow * 2 + 1 - fast}
    over_slow = {"dp": (1 - slow) * 2 + fast}
    over_col = [{"ecol": lax.rem(col + shift, n_col)} for shift in range(1, n_col)]
    greet([over_row, over_fast, over_slow] + over_col)
    flying = {}

    def launch(at, number, source, target, device):
        copy = remote(source, target, send_sems.at[at, number], recv_sems.at[at, number], device)
        copy.start()
        flying[at, number] = copy

    def parts(at):
        width = widths[at]
        if width >= 2 * LANES:
            return ((0, 0, width // 2), (1, width // 2, width // 2))
        return ((0, 0, width),)

    def step(at, stage):
        from_row, row_sum, from_near, near_sum, from_far, far_sum, from_col = held[at]
        if stage == 0:
            launch(at, 0, grads[at].at[:, :, 1 - row], from_row, over_row)
        elif stage == 1:
            flying[at, 0].wait()
            for high in range(2):
                for low in range(2):
                    row_sum[high, low] = (
                        grads[at][high, low, row].astype(jnp.float32)
                        + from_row[high, low].astype(jnp.float32)
                    ).astype(row_sum.dtype)
            for which, start, width in parts(at):
                cut = pl.ds(start, width)
                if which == 0:
                    launch(at, 1, row_sum.at[:, 1 - fast, :, cut], from_near.at[:, :, cut], over_fast)
                else:
                    launch(at, 2, row_sum.at[1 - slow, :, :, cut], from_near.at[:, :, cut], over_slow)
        elif stage == 2:
            for which, start, width in parts(at):
                cut = pl.ds(start, width)
                flying[at, 1 + which].wait()
                for place in range(2):
                    if which == 0:
                        kept = row_sum[place, fast, :, cut]
                    else:
                        kept = row_sum[slow, place, :, cut]
                    near_sum[place, :, cut] = (
                        kept.astype(jnp.float32) + from_near[place, :, cut].astype(jnp.float32)
                    ).astype(near_sum.dtype)
                if which == 0:
                    launch(at, 3, near_sum.at[1 - slow, :, cut], from_far.at[:, cut], over_slow)
                else:
                    launch(at, 4, near_sum.at[1 - fast, :, cut], from_far.at[:, cut], over_fast)
        elif stage == 3:
            for which, start, width in parts(at):
                cut = pl.ds(start, width)
                flying[at, 3 + which].wait()
                kept = near_sum[slow if which == 0 else fast, :, cut]
                total = kept.astype(jnp.float32) + from_far[:, cut].astype(jnp.float32)
                far_sum[:, :, cut] = total.reshape(n_col, depth, width).astype(far_sum.dtype)
            for shift in range(1, n_col):
                peer = lax.rem(col + shift, n_col)
                launch(at, 4 + shift, far_sum.at[peer], from_col.at[shift - 1], over_col[shift - 1])
        else:
            total = far_sum[col].astype(jnp.float32)
            for shift in range(1, n_col):
                flying[at, 4 + shift].wait()
                total = total + from_col[shift - 1].astype(jnp.float32)
            totals[at][...] = total

    for turn in range(count + 4):
        for at in range(count):
            if 0 <= turn - at <= 4:
                step(at, turn - at)


def reduce_shares(grads, sizes, number):
    n_dp, n_row, n_col = sizes
    depth = grads[0].shape[0] // (n_dp * n_row * n_col)
    strip = n_col * depth
    widths = tuple(grad.shape[1] for grad in grads)
    shaped = [grad.reshape(2, 2, n_row, strip, grad.shape[1]) for grad in grads]
    scratch = []
    for grad in grads:
        kind, width = grad.dtype, grad.shape[1]
        late = kind if depth % 16 == 0 else jnp.float32
        scratch += [
            pltpu.VMEM((2, 2, strip, width), kind),
            pltpu.VMEM((2, 2, strip, width), kind),
            pltpu.VMEM((2, strip, width), kind),
            pltpu.VMEM((2, strip, width), kind),
            pltpu.VMEM((strip, width), kind),
            pltpu.VMEM((n_col, depth, width), late),
            pltpu.VMEM((n_col - 1, depth, width), late),
        ]
    sems = (len(grads), 4 + n_col)
    return pl.pallas_call(
        functools.partial(reduce_kernel, (n_dp, n_row, n_col, depth), widths),
        out_shape=[jax.ShapeDtypeStruct((depth, width), jnp.float32) for width in widths],
        in_specs=[pl.BlockSpec(memory_space=pltpu.VMEM)] * len(grads),
        out_specs=[pl.BlockSpec(memory_space=pltpu.VMEM)] * len(grads),
        scratch_shapes=scratch + [pltpu.SemaphoreType.DMA(sems), pltpu.SemaphoreType.DMA(sems)],
        compiler_params=pltpu.CompilerParams(
            collective_id=number, has_side_effects=True, vmem_limit_bytes=VMEM_LIMIT
        ),
    )(*shaped)


def gelu_parts(gate_part):
    inner = 0.7978845608028654 * (gate_part + 0.044715 * gate_part * gate_part * gate_part)
    bend = jnp.tanh(inner)
    value = 0.5 * gate_part * (1.0 + bend)
    slope = 0.5 * (1.0 + bend) + 0.5 * gate_part * (1.0 - bend * bend) * 0.7978845608028654 * (
        1.0 + 3.0 * 0.044715 * gate_part * gate_part
    )
    return value, slope


def split_scalar(values):
    high = lax.reduce_precision(values, 8, 7)
    low = values - high
    panel = jnp.concatenate([high, low], axis=1)
    return rounded(jnp.pad(panel, ((0, 0), (0, LANES - 2))))


def join_scalar(panel):
    return panel[:, 0:1].astype(jnp.float32) + panel[:, 1:2].astype(jnp.float32)


def expert_parts(rows, picks, down_rows, gate_mat, up_mat):
    gate_part = product(rows, gate_mat)
    up_part = product(rows, up_mat)
    value, slope = gelu_parts(gate_part)
    hidden = value * up_part
    back = picks * down_rows
    gate_back = rounded(back * up_part * slope)
    up_back = rounded(back * value)
    return hidden, gate_back, up_back


def body(
    tokens,
    lengths,
    routes,
    attn_gain,
    query_weight,
    key_weight,
    value_weight,
    out_weight,
    relative_bias,
    moe_gain,
    router_weight,
    gate_weight,
    up_weight,
    down_weight,
    cotangent,
):
    tok_rows = tokens.shape[1]
    width = tokens.shape[2]
    head_count, bucket_count = relative_bias.shape
    head_size = width // head_count
    expert_count = router_weight.shape[1]
    capacity = 5 * tok_rows // (2 * expert_count)
    room = -(-capacity // 16) * 16
    n_dp, n_row, n_col = (lax.axis_size(name) for name in ("dp", "erow", "ecol"))
    group = n_row * n_col
    slot_count = expert_count * room
    piece = lax.axis_index("erow")
    replica = lax.axis_index("dp")
    inputs = tokens[0].astype(jnp.float32)
    seq_length = lengths[0]
    gate_mat, up_mat, down_mat = gate_weight[0], up_weight[0], down_weight[0]
    hidden_width = gate_mat.shape[1]

    query_pos = piece * tok_rows + jnp.arange(tok_rows, dtype=jnp.int32)
    key_pos = jnp.concatenate([query_pos, query_pos + (1 - 2 * piece) * tok_rows])
    bucket_ids = bucket_of(key_pos[None, :] - query_pos[:, None])
    bias_onehot = (
        jnp.arange(bucket_count, dtype=jnp.int32)[:, None, None] == bucket_ids[None]
    ).astype(jnp.bfloat16)
    bias_full = jnp.einsum(
        "zt,tyx->zyx", relative_bias, bias_onehot, precision=highest, preferred_element_type=jnp.float32
    )
    key_live = key_pos < seq_length
    tok_live = query_pos < seq_length
    pair_routes = routes[0]
    route_flat = pair_routes.reshape(-1)
    pair_live = jnp.broadcast_to(tok_live[:, None], pair_routes.shape).reshape(-1)
    expert_range = jnp.arange(expert_count, dtype=jnp.int32)
    route_hot = ((route_flat[:, None] == expert_range[None, :]) & pair_live[:, None]).astype(jnp.int32)
    earlier = jnp.cumsum(route_hot, axis=0) - route_hot
    position = jnp.sum(earlier * route_hot, axis=1)
    kept_pairs = pair_live & (position < capacity)
    slot_ids = jnp.where(kept_pairs, route_flat * room + position, -1).reshape(tok_rows, 2)
    slot_range = jnp.arange(slot_count, dtype=jnp.int32)
    select_lead = (slot_ids[:, 0:1] == slot_range[None, :]).astype(jnp.bfloat16)
    select_trail = (slot_ids[:, 1:2] == slot_range[None, :]).astype(jnp.bfloat16)
    select_both = select_lead + select_trail
    choice_hot = (pair_routes[:, :, None] == expert_range[None, None, :]).astype(jnp.float32)

    def sent(rows, number):
        return exchange(rows.reshape(group, room, rows.shape[1]), (n_row, n_col), number).reshape(
            rows.shape
        )

    out_grad_low = cotangent[0]
    out_grad = out_grad_low.astype(jnp.float32)
    got_grads = sent(rounded(product_left(select_both, out_grad_low)), 0)
    all_grads = replicas(got_grads)
    down_rows = product_back(all_grads, down_mat)

    normed = rounded(rms_scale(inputs, attn_gain))
    queries = rounded(product(normed, query_weight))
    both_local = jnp.concatenate(
        [rounded(product(normed, key_weight)), rounded(product(normed, value_weight))], axis=1
    )
    both_other = lax.ppermute(both_local, "erow", [(0, 1), (1, 0)])
    both_all = jnp.concatenate([both_local, both_other], axis=0)
    seq_rows = both_all.shape[0]
    query_heads = queries.reshape(tok_rows, head_count, head_size)
    key_heads = both_all[:, :width].reshape(seq_rows, head_count, head_size)
    value_heads = both_all[:, width:].reshape(seq_rows, head_count, head_size)
    scores = (
        jnp.einsum("qhd,khd->hqk", query_heads, key_heads, preferred_element_type=jnp.float32) * 0.125
        + bias_full
    )
    scores = jnp.where(key_live[None, None, :], scores, -1000000000.0)
    attn_probs = jax.nn.softmax(scores, axis=-1)
    probs_low = rounded(attn_probs)
    mixed = rounded(
        jnp.einsum("hqk,khd->qhd", probs_low, value_heads, preferred_element_type=jnp.float32).reshape(
            tok_rows, width
        )
    )
    residual = inputs + product(mixed, out_weight)
    moe_in = rms_scale(residual, moe_gain)
    gate_probs = jax.nn.softmax(jnp.dot(moe_in, router_weight, precision=highest), axis=-1)
    gate_pick = jnp.sum(gate_probs[:, None, :] * choice_hot, axis=-1)

    slot_pick = lax.dot_general(
        select_lead.astype(jnp.float32), gate_pick[:, 0:1], (((0,), (0,)), ((), ())), precision=highest
    ) + lax.dot_general(
        select_trail.astype(jnp.float32), gate_pick[:, 1:2], (((0,), (0,)), ((), ())), precision=highest
    )
    slot_rows = rounded(product_left(select_both, rounded(moe_in)))
    got = sent(jnp.concatenate([slot_rows, split_scalar(slot_pick)], axis=1), 1)
    all_got = replicas(got)
    own_rows, own_picks = got[:, :width], join_scalar(got[:, width:])
    hidden, gate_back, up_back = expert_parts(
        own_rows, own_picks, down_rows[: got.shape[0]], gate_mat, up_mat
    )
    pick_slots = jnp.sum(hidden * down_rows[: got.shape[0]], axis=1, keepdims=True)
    row_back = rounded(product_back(gate_back, gate_mat) + product_back(up_back, up_mat))
    back = sent(jnp.concatenate([row_back, split_scalar(pick_slots)], axis=1), 2)
    expert_out = rounded(product(rounded(hidden), down_mat))
    out_slots = sent(expert_out, 3)
    output = rounded(
        residual
        + gate_pick[:, 0:1] * product(select_lead, out_slots)
        + gate_pick[:, 1:2] * product(select_trail, out_slots)
    )

    slot_pick_back = join_scalar(back[:, width:])
    pick_back = jnp.concatenate(
        [
            jnp.dot(select_lead.astype(jnp.float32), slot_pick_back, precision=highest),
            jnp.dot(select_trail.astype(jnp.float32), slot_pick_back, precision=highest),
        ],
        axis=1,
    )
    prob_back = jnp.sum(pick_back[:, :, None] * choice_hot, axis=1)
    logit_back = gate_probs * (prob_back - jnp.sum(gate_probs * prob_back, axis=-1, keepdims=True))
    router_grad = lax.dot_general(moe_in, logit_back, (((0,), (0,)), ((), ())), precision=highest)
    moe_back = product(select_both, back[:, :width]) + lax.dot_general(
        logit_back, router_weight, (((1,), (1,)), ((), ())), precision=highest
    )
    _, moe_pull = jax.vjp(rms_scale, residual, moe_gain)
    residual_part, moe_gain_grad = moe_pull(moe_back)
    residual_grad = out_grad + residual_part
    branch_grad = rounded(residual_grad)
    out_wgrad = product_left(mixed, branch_grad)
    mixed_grad = rounded(product_back(branch_grad, out_weight)).reshape(tok_rows, head_count, head_size)

    prob_part = jnp.einsum("qhd,khd->hqk", mixed_grad, value_heads, preferred_element_type=jnp.float32)
    score_back = rounded(
        attn_probs * (prob_part - jnp.sum(attn_probs * prob_part, axis=-1, keepdims=True))
    )
    query_grad = rounded(
        jnp.einsum("hqk,khd->qhd", score_back, key_heads, preferred_element_type=jnp.float32) * 0.125
    ).reshape(tok_rows, width)
    key_part = (
        jnp.einsum("hqk,qhd->khd", score_back, query_heads, preferred_element_type=jnp.float32) * 0.125
    ).reshape(seq_rows, width)
    value_part = jnp.einsum(
        "hqk,qhd->khd", probs_low, mixed_grad, preferred_element_type=jnp.float32
    ).reshape(seq_rows, width)
    both_part = jnp.concatenate([key_part, value_part], axis=1)
    far_part = lax.ppermute(rounded(both_part[tok_rows:]), "erow", [(0, 1), (1, 0)])
    both_grad = rounded(both_part[:tok_rows] + far_part.astype(jnp.float32))
    key_grad, value_grad = both_grad[:, :width], both_grad[:, width:]
    bias_grad = jnp.einsum("tlx,mlx->tm", score_back, bias_onehot, preferred_element_type=jnp.float32)
    normed_grad = (
        product_back(query_grad, query_weight)
        + product_back(key_grad, key_weight)
        + product_back(value_grad, value_weight)
    )
    _, attn_pull = jax.vjp(rms_scale, inputs, attn_gain)
    input_part, attn_gain_grad = attn_pull(normed_grad)
    token_grad = residual_grad + input_part

    width_share, hidden_share = width // n_dp, hidden_width // n_dp
    all_rows, all_picks = all_got[:, :width], join_scalar(all_got[:, width:])
    all_hidden, all_gate_back, all_up_back = expert_parts(
        all_rows, all_picks, down_rows, gate_mat, up_mat
    )
    rows_part = lax.dynamic_slice_in_dim(all_rows, replica * width_share, width_share, 1)
    hidden_part = lax.dynamic_slice_in_dim(
        rounded(all_picks * all_hidden), replica * hidden_share, hidden_share, 1
    )
    gate_total = product_left(rows_part, all_gate_back)
    up_total = product_left(rows_part, all_up_back)
    down_total = product_left(hidden_part, all_grads)

    device_count = n_dp * n_row * n_col
    bias_column = jnp.pad(
        bias_grad.reshape(device_count, -1),
        ((0, 0), (0, (width - head_count * bucket_count) // device_count)),
    ).reshape(-1, 1)
    small = jnp.concatenate([attn_gain_grad[:, None], moe_gain_grad[:, None], bias_column, router_grad], axis=1)
    small = jnp.pad(small, ((0, 0), (0, LANES - small.shape[1])))
    wgrads = [rounded(out_wgrad)] + [
        rounded(product_left(normed, grad)) for grad in (query_grad, key_grad, value_grad)
    ]
    out_sum, query_sum, key_sum, value_sum, small_sum = reduce_shares(
        wgrads + [small], (n_dp, n_row, n_col), 4
    )
    bias_share = head_count * bucket_count // device_count
    return (
        output[None],
        token_grad[None],
        small_sum[:, 0],
        query_sum,
        key_sum,
        value_sum,
        out_sum,
        small_sum[:bias_share, 2],
        small_sum[:, 1],
        small_sum[:, 3 : 3 + expert_count],
        gate_total[None],
        up_total[None],
        down_total[None],
    )


def solution(mesh):
    rows = P(("dp", "ecol"), "erow", None)
    experts = P(("erow", "ecol"), None, None)
    every = ("dp", "erow", "ecol")
    shares = P(("erow", "ecol"), "dp", None)
    return jax.shard_map(
        body,
        mesh=mesh,
        in_specs=(
            (rows, P(("dp", "ecol")), rows) + (P(),) * 8 + (experts, experts, experts, rows)
        ),
        out_specs=(rows, rows, P(every))
        + (P(every, None),) * 4
        + (P(every), P(every), P(every, None), shares, shares, shares),
        check_vma=False,
    )
```

time: 1170 us -> 626 us (0.54)
  waiting for transfers between devices: 659 us -> 25.2 us
  Pallas kernels: 0 us -> 200 us
  blocking collectives: 132 us -> 0 us
  local copies, waits for them, and re-layouts: 28.1 us -> 51.3 us
  between operations: 15.6 us -> 2.79 us
    reduce_scatter x6 -> x0, waiting for transfers between devices: 475 us -> none  [the longest x1 149 us: body(): lax.psum_scatter(value_wgrad, ('dp', 'erow', 'ecol'), scatter_dimension=0...]
    pallas_call x0 -> x5, Pallas kernels: none -> 200 us  [the longest x4 136 us: exchange(): pl.pallas_call(functools.partial(exchange_kernel, sizes), out_shape=jax.S...]
    all_to_all x6 -> x0, blocking collectives: 91.8 us -> none  [the longest x1 38.1 us: send_rows(): lax.all_to_all(lax.all_to_all(sectioned_form(block_rows, capacity), 'erow...]
    unnamed x12 -> x0, waiting for transfers between devices: 65.4 us -> none
    all_to_all x2 -> x0, waiting for transfers between devices: 61.1 us -> none  [the longest x1 30.8 us: return_rows(): lax.all_to_all(lax.all_to_all(sectioned_form(block_rows, capacity), 'erow...]
    all_gather x4 -> x0, waiting for transfers between devices: 57.7 us -> none  [the longest x1 57.7 us: body(): rows_piece = lax.all_gather(received, 'dp', axis=0, tiled=True)]
    unnamed x1 -> x0, blocking collectives: 40.2 us -> none
    ppermute x0 -> x10, waiting for transfers between devices: none -> 25.2 us  [the longest x2 25.1 us: replicas(): upper = lax.ppermute(by_first[:half], 'dp', second)]
  transfers between devices with their start and end apart: 13 -> 10, of which waited for: 8 -> 1; matrix products, arithmetic and copies ran while one was open for 22% -> 38% of each run, Pallas kernels for 0% -> 27%
where the time goes in v1:
time: 626 us; the launch traced here: 619 us
  matrix products  306 us (49%)
  Pallas kernels  200 us (32%)
  local copies, waits for them, and re-layouts  51.3 us (8%)
  waiting for transfers between devices  25.2 us (4%)
  other arithmetic  23.6 us (4%)
  starting transfers between devices  9.34 us (1%)
    pallas_call x4, Pallas kernels, exchange(): pl.pallas_call(functools.partial(exchange_kernel, sizes), out_shape=jax.S...  136 us
    dot_general x12, matrix products, product(): return jnp.dot(left_side, right_side, preferred_element_type=jnp.float32)  98.7 us
    dot_general x9, matrix products, product_left(): lax.dot_general(left_side, right_side, (((0,), (0,)), ((), ())), preferre...  88 us
    pallas_call x1, Pallas kernels, reduce_shares(): pl.pallas_call(functools.partial(reduce_kernel, (n_dp, n_row, n_col, dept...  64 us
    dot_general x7, matrix products, product_back(): lax.dot_general(left_side, right_side, (((1,), (1,)), ((), ())), preferre...  54 us
    ppermute x2, waiting for transfers between devices, replicas(): upper = lax.ppermute(by_first[:half], 'dp', second)  25.1 us
    unnamed x133, local copies, waits for them, and re-layouts  24.9 us
    dot_general x1, matrix products, body(): jnp.einsum('hqk,qhd->khd', probs_low, mixed_grad, preferred_element_type=...  14.8 us
  transfers between devices with their start and end apart: 10, of which 1 were waited for; matrix products, arithmetic and copies ran while one was open for 38% of the time, Pallas kernels for 27%

profile of v1, /device:TPU:0, one launch (start us, length us, event | category | flops | bytes accessed | tf_op | source)
XLA Modules:
  0.0 618.7 jit_solution(3265727985134940062)
XLA Ops:
  5.2 2.8 convolution_convert_fusion.4
  8.0 31.7 %shard_map.248 = bf16[8,80,1024]{2,1,0:T(8,128)(2,1)} custom-call(bf16[8,80,1024]{2,1,0:T(8,128)(2,1)} %bitcast.206), custom_call_target="tpu_custom_call" | custom-call | tf_op jit(solution)/shard_map/pallas_call | solution.py:91
  47.9 3.1 convolution_convert_fusion.7
  56.4 7.3 %fusion.9 = f32[256,512,16]{1,2,0:T(8,128)} fusion(s32[256,512]{1,0:T(8,128)S(1)} %fusion.125, f32[16,32]{1,0:T(8,128)S(1)} %copy-done.49), kind=kOutput, calls=%fused_computation.14 | convolution fusion | flops 809500672 | bytes 8914944 | tf_op jit(solution)/shard_map/zt,tyx->zyx/dot_general | solution.py:303
  68.4 9.5 %fusion.14 = f32[16,256,512]{2,1,0:T(8,128)S(1)} fusion(f32[256,512,16]{1,2,0:T(8,128)} %fusion.9, pred[512]{0:T(512)(128)(4,1)S(1)} %broadcast_compare_fusion, bf16[256,16,64]{0,2,1:T(8,128)(2,1)} %bitcast.197, bf16[512,16,64]{0,2,1:T(8,128)(2,1)S(1)} %bitcast.176), kind=kOutput, calls=%fused_computation.21 | convolution fusion | flops 274726912 | bytes 18350592 | tf_op jit(solution)/shard_map/qhd,khd->hqk/dot_general | solution.py:346
  77.9 4.9 fusion.201
  85.2 14.5 %fusion.87 = bf16[16,64,256]{2,1,0:T(8,128)(2,1)} fusion(bf16[512,16,64]{0,2,1:T(8,128)(2,1)S(1)} %bitcast.207, f32[16,256]{1,0:T(8,128)S(1)} %get-tuple-element.106, f32[16,256,512]{2,1,0:T(8,128)} %copy-done.2), kind=kOutput, calls=%fused_computation.115 | convolution fusion | flops 274993664 | bytes 9977856 | tf_op jit(solution)/shard_map/hqk,khd->qhd/dot_general | solution.py:353
  99.7 2.7 multiply_reduce_fusion.4
  106.5 35.6 %shard_map.246 = bf16[8,80,1152]{2,1,0:T(8,128)(2,1)} custom-call(bf16[8,80,1152]{2,1,0:T(8,128)(2,1)} %bitcast.190), custom_call_target="tpu_custom_call" | custom-call | tf_op jit(solution)/shard_map/pallas_call | solution.py:91
  143.2 2.6 constant_dynamic-update-slice_fusion.9
  148.7 9.8 %fusion.40 = f32[640,2816]{1,0:T(8,128)} fusion(bf16[1,1024,2816]{2,1,0:T(8,128)(2,1)} %param.26, bf16[640,1152]{1,0:T(8,128)(2,1)} %bitcast.187), kind=kOutput, calls=%fused_computation.55 | convolution fusion | flops 3690987520 | bytes 14286848 | tf_op jit(solution)/shard_map/dot_general | solution.py:35
  164.9 25.1 %collective-permute-done.3 = bf16[320,1024]{1,0:T(8,128)(2,1)S(1)} collective-permute-done((bf16[320,1024]{1,0:T(8,128)(2,1)S(1)}, bf16[320,1024]{1,0:T(8,128)(2,1)S(1)}, u32[]{:S(2)}, u32[]{:S(2)}) %collective-permute-start.3) | collective-permute-done | bytes 655392 | tf_op jit(solution)/shard_map/ppermute | solution.py:111
  190.2 23.3 %fusion.26 = f32[2560,2816]{1,0:T(8,128)} fusion(bf16[2560,1024]{1,0:T(8,128)(2,1)S(1)} %constant_dynamic-update-slice_fusion, bf16[1,2816,1024]{2,1,0:T(8,128)(2,1)} %param.28), kind=kOutput, calls=%fused_computation.41 | convolution fusion | flops 14763950080 | bytes 39845888 | tf_op jit(solution)/shard_map/dot_general | solution.py:39
  213.4 11.2 %multiply_reduce_fusion.1 = (f32[640]{0:T(1024)S(1)}, f32[640,2816]{1,0:T(8,128)}) fusion(f32[2560,2816]{1,0:T(8,128)} %fusion.26, f32[640,2816]{1,0:T(8,128)} %fusion.40, bf16[1,1024,2816]{2,1,0:T(8,128)(2,1)} %param.27, bf16[640,1152]{1,0:T(8,128)(2,1)S(1)} %bitcast.189), kind=kOutput, calls=%fused_computation.37 | convolution fusion | flops 3710811648 | bytes 28707328 | tf_op jit(solution)/shard_map/dot_general | solution.py:35
  224.6 11.0 %fusion.32 = f32[640,1024]{1,0:T(8,128)} fusion(bf16[1,1024,2816]{2,1,0:T(8,128)(2,1)} %param.27, f32[2560,2816]{1,0:T(8,128)} %fusion.26, f32[640]{0:T(1024)S(1)} %add_reduce_fusion.1, f32[640,2816]{1,0:T(8,128)} %fusion.40), kind=kOutput, calls=%fused_computation.47 | convolution fusion | flops 3710812160 | bytes 22809088 | tf_op jit(solution)/shard_map/dot_general | solution.py:39
  235.8 14.6 %add_convert_fusion = bf16[640,1024]{1,0:T(8,128)(2,1)S(1)} fusion(f32[640,1024]{1,0:T(8,128)} %fusion.32, bf16[1,1024,2816]{2,1,0:T(8,128)(2,1)} %param.26, f32[640,2816]{1,0:T(8,128)} %fusion.40, f32[640,2816]{1,0:T(8,128)} %get-tuple-element.113, f32[2560,2816]{1,0:T(8,128)} %fusion.26, f32[640]{0:T(1024)S(1)} %add_reduce_fusion.1), kind=kOutput, calls=%fused_computation.71 | convolution fusion | flops 3730145280 | bytes 31328768 | tf_op jit(solution)/shard_map/dot_general | solution.py:39
  251.6 36.1 %shard_map.249 = bf16[8,80,1152]{2,1,0:T(8,128)(2,1)} custom-call(bf16[8,80,1152]{2,1,0:T(8,128)(2,1)} %bitcast.191), custom_call_target="tpu_custom_call" | custom-call | tf_op jit(solution)/shard_map/pallas_call | solution.py:91
  301.9 14.8 %fusion.60 = f32[16,64,512]{2,1,0:T(8,128)} fusion(bf16[256,16,64]{0,2,1:T(8,128)(2,1)} %bitcast.209, f32[16,256]{1,0:T(8,128)S(1)} %get-tuple-element.106, f32[16,256,512]{2,1,0:T(8,128)} %copy-done.2), kind=kOutput, calls=%fused_computation.78 | convolution fusion | flops 274731520 | bytes 11026432 | tf_op jit(solution)/shard_map/hqk,qhd->khd/dot_general | solution.py:416
  316.7 5.9 multiply_reduce_fusion
  322.6 4.6 multiply_convert_fusion.2
  330.6 4.2 fusion.98
  334.9 8.9 %fusion.71 = bf16[640,1024]{1,0:T(8,128)(2,1)} fusion(bf16[1,2816,1024]{2,1,0:T(8,128)(2,1)S(1)} %bitcast.218, f32[640,2816]{1,0:T(8,128)} %get-tuple-element.113, f32[640,2816]{1,0:T(8,128)S(1)} %bitcast.220), kind=kOutput, calls=%fused_computation.90 | convolution fusion | flops 3709665280 | bytes 21495808 | tf_op jit(solution)/shard_map/dot_general | solution.py:35
  344.9 33.1 %shard_map.247 = bf16[8,80,1024]{2,1,0:T(8,128)(2,1)} custom-call(bf16[8,80,1024]{2,1,0:T(8,128)(2,1)} %bitcast.205), custom_call_target="tpu_custom_call" | custom-call | tf_op jit(solution)/shard_map/pallas_call | solution.py:91
  378.0 2.9 convolution_multiply_fusion.1
  381.1 3.2 fusion.93
  384.3 3.4 convolution_convert_fusion.2
  412.9 64.0 %shard_map.250 = (f32[32,1024]{1,0:T(8,128)}, f32[32,1024]{1,0:T(8,128)}, f32[32,1024]{1,0:T(8,128)}, f32[32,1024]{1,0:T(8,128)}, f32[32,128]{1,0:T(8,128)}) custom-call(bf16[2,2,2,128,1024]{4,3,2,1,0:T(8,128)(2,1)} %bitcast.178, bf16[2,2,2,128,1024]{4,3,2,1,0:T(8,128)(2,1)} %bitcast.181, bf16[2,2,2,128,1024]{4,3,2,1,0:T(8,128)(2,1)} %bitcast.182, ...), custom_call_target="tpu_custom_call" | custom-call | tf_op jit(solution)/shard_map/pallas_call | solution.py:219
  485.6 29.1 %multiply_multiply_fusion.1 = (f32[2560,2816]{1,0:T(8,128)}, f32[2560,2816]{1,0:T(8,128)}) fusion(bf16[1,1024,2816]{2,1,0:T(8,128)(2,1)} %param.26, bf16[2560,1152]{1,0:T(8,128)(2,1)} %constant_dynamic-update-slice_fusion.5), kind=kOutput, calls=%fused_computation.11 | convolution fusion | flops 14821621760 | bytes 68681728 | tf_op jit(solution)/shard_map/dot_general | solution.py:35
  514.7 22.5 %fusion.30 = f32[2560,2816]{1,0:T(8,128)} fusion(bf16[1,1024,2816]{2,1,0:T(8,128)(2,1)} %param.27, bf16[2560,1152]{1,0:T(8,128)(2,1)} %constant_dynamic-update-slice_fusion.5), kind=kOutput, calls=%fused_computation.45 | convolution fusion | flops 14763950080 | bytes 39845888 | tf_op jit(solution)/shard_map/dot_general | solution.py:35
  540.9 23.6 %fusion.43 = f32[1,256,2816]{2,1,0:T(8,128)} fusion(f32[2560,2816]{1,0:T(8,128)} %fusion.26, f32[2560]{0:T(1024)S(1)} %add_reduce_fusion, bf16[2560,1024]{1,0:T(8,128)(2,1)S(1)} %slice.155, s32[]{:T(128)S(6)} %select_n.35, f32[2560,2816]{1,0:T(8,128)} %get-tuple-element.119), kind=kOutput, calls=%fused_computation.61 | convolution fusion | flops 3770286080 | bytes 61878276 | tf_op jit(solution)/shard_map/dot_general | solution.py:45
  564.5 34.7 %fusion.44 = f32[1,256,2816]{2,1,0:T(8,128)} fusion(f32[2560,2816]{1,0:T(8,128)} %get-tuple-element.119, f32[2560,2816]{1,0:T(8,128)} %fusion.30, f32[2560,2816]{1,0:T(8,128)} %fusion.26, f32[2560]{0:T(1024)S(1)} %add_reduce_fusion, bf16[2560,1024]{1,0:T(8,128)(2,1)} %copy-done.17, s32[]{:T(128)S(6)} %select_n.35), kind=kOutput, calls=%fused_computation.62 | convolution fusion | flops 3842375680 | bytes 90712064 | tf_op jit(solution)/shard_map/dot_general | solution.py:45
  599.3 16.3 %fusion.64 = f32[1,704,1024]{2,1,0:T(8,128)} fusion(bf16[2560,1024]{1,0:T(8,128)(2,1)} %copy-done.30, f32[2560,2816]{1,0:T(8,128)} %fusion.30, s32[]{:T(128)S(6)} %select_n.36, f32[2560,2816]{1,0:T(8,128)} %get-tuple-element.118, f32[2560]{0:T(1024)S(1)} %add_reduce_fusion), kind=kOutput, calls=%fused_computation.86 | convolution fusion | flops 3696394240 | bytes 23865348 | tf_op jit(solution)/shard_map/dot_general | solution.py:45
  (247 shorter events, 98.9 us)
Async XLA Ops:
  0.6 42.3 %copy-start = (bf16[1024,1024]{1,0:T(8,128)(2,1)S(1)}, bf16[1024,1024]{1,0:T(8,128)(2,1)}, u32[]{:S(2)}) copy-start(bf16[1024,1024]{1,0:T(8,128)(2,1)} %param.21) | copy-start | bytes 6291460
  0.7 42.1 %copy-start.5 = (bf16[1,256,1024]{2,1,0:T(8,128)(2,1)S(1)}, bf16[1,256,1024]{2,1,0:T(8,128)(2,1)}, u32[]{:S(2)}) copy-start(bf16[1,256,1024]{2,1,0:T(8,128)(2,1)} %param.15) | copy-start | bytes 1572868
  0.7 42.3 %copy-start.37 = (f32[1024]{0:T(1024)S(1)}, f32[1024]{0:T(1024)}, u32[]{:S(2)}) copy-start(f32[1024]{0:T(1024)} %param.18) | copy-start | bytes 12292
  5.2 99.3 %copy-start.41 = (s32[256]{0:T(256)}, s32[256]{0:T(256)S(1)}, u32[]{:S(2)}) copy-start(s32[256]{0:T(256)S(1)} %get-tuple-element.93) | copy-start | bytes 3076
  5.2 99.3 %copy-start.43 = (s32[256]{0:T(256)}, s32[256]{0:T(256)S(1)}, u32[]{:S(2)}) copy-start(s32[256]{0:T(256)S(1)} %get-tuple-element.92) | copy-start | bytes 3076
  39.6 106.2 %collective-permute-start.1 = (bf16[640,1024]{1,0:T(8,128)(2,1)}, bf16[640,1024]{1,0:T(8,128)(2,1)}, u32[]{:S(2)}, u32[]{:S(2)}) collective-permute-start(bf16[640,1024]{1,0:T(8,128)(2,1)} %bitcast.192), channel_id=1, source_target_pairs={{0,8},{8,0},{16,24},{24,16},{1,9},{9,1},{17,25},{25,17},{2,10},{10... | collective-permute-start | bytes 3932168 | tf_op jit(solution)/shard_map/ppermute | solution.py:109
  41.2 117.4 %collective-permute-start.2 = (bf16[640,1024]{1,0:T(8,128)(2,1)}, bf16[640,1024]{1,0:T(8,128)(2,1)}, u32[]{:S(2)}, u32[]{:S(2)}) collective-permute-start(bf16[640,1024]{1,0:T(8,128)(2,1)} %bitcast.193), channel_id=1, source_target_pairs={{0,16},{8,24},{16,0},{24,8},{1,17},{9,25},{17,1},{25,9},{2,18},{10... | collective-permute-start | bytes 3932168 | tf_op jit(solution)/shard_map/ppermute | solution.py:110
  47.9 15.8 %collective-permute-start = (bf16[256,2048]{1,0:T(8,128)(2,1)}, bf16[256,2048]{1,0:T(8,128)(2,1)}, u32[]{:S(2)}, u32[]{:S(2)}) collective-permute-start(bf16[256,2048]{1,0:T(8,128)(2,1)} %pad_maximum_fusion.2), channel_id=1, source_target_pairs={{0,4},{4,0},{1,5},{5,1},{2,6},{6,2},{3,7},{7,3},{8,12},{12,8},{9,1... | collective-permute-start | bytes 3145736 | tf_op jit(solution)/shard_map/ppermute | solution.py:339
  85.2 17.2 %copy-start.31 = (f32[1024,8]{0,1:T(8,128)S(1)}, f32[1024,8]{0,1:T(8,128)}, u32[]{:S(2)}) copy-start(f32[1024,8]{0,1:T(8,128)} %param.25) | copy-start | bytes 98308
  85.2 17.2 %copy-start.36 = (f32[1024]{0:T(1024)S(1)}, f32[1024]{0:T(1024)}, u32[]{:S(2)}) copy-start(f32[1024]{0:T(1024)} %param.24) | copy-start | bytes 12292
  103.4 42.4 %copy-start.48 = (f32[256]{0:T(256)}, f32[256]{0:T(256)S(1)}, u32[]{:S(2)}) copy-start(f32[256]{0:T(256)S(1)} %fusion.164) | copy-start | bytes 3076
  142.1 249.5 %collective-permute-start.6 = (bf16[640,1152]{1,0:T(8,128)(2,1)}, bf16[640,1152]{1,0:T(8,128)(2,1)}, u32[]{:S(2)}, u32[]{:S(2)}) collective-permute-start(bf16[640,1152]{1,0:T(8,128)(2,1)} %bitcast.184), channel_id=1, source_target_pairs={{0,8},{8,0},{16,24},{24,16},{1,9},{9,1},{17,25},{25,17},{2,10},{10... | collective-permute-start | bytes 4423688 | tf_op jit(solution)/shard_map/ppermute | solution.py:109
  142.7 251.5 %collective-permute-start.7 = (bf16[640,1152]{1,0:T(8,128)(2,1)}, bf16[640,1152]{1,0:T(8,128)(2,1)}, u32[]{:S(2)}, u32[]{:S(2)}) collective-permute-start(bf16[640,1152]{1,0:T(8,128)(2,1)} %bitcast.185), channel_id=1, source_target_pairs={{0,16},{8,24},{16,0},{24,8},{1,17},{9,25},{17,1},{25,9},{2,18},{10... | collective-permute-start | bytes 4423688 | tf_op jit(solution)/shard_map/ppermute | solution.py:110
  147.1 42.9 %collective-permute-start.3 = (bf16[320,1024]{1,0:T(8,128)(2,1)S(1)}, bf16[320,1024]{1,0:T(8,128)(2,1)S(1)}, u32[]{:S(2)}, u32[]{:S(2)}) collective-permute-start(bf16[320,1024]{1,0:T(8,128)(2,1)S(1)} %slice.143), channel_id=1, source_target_pairs={{0,16},{8,24},{16,0},{24,8},{1,17},{9,25},{17,1},{25,9},{2,18},{10... | collective-permute-start | bytes 1966088 | tf_op jit(solution)/shard_map/ppermute | solution.py:111
  159.7 30.4 %collective-permute-start.4 = (bf16[320,1024]{1,0:T(8,128)(2,1)S(1)}, bf16[320,1024]{1,0:T(8,128)(2,1)S(1)}, u32[]{:S(2)}, u32[]{:S(2)}) collective-permute-start(bf16[320,1024]{1,0:T(8,128)(2,1)S(1)} %slice.144), channel_id=1, source_target_pairs={{0,8},{8,0},{16,24},{24,16},{1,9},{9,1},{17,25},{25,17},{2,10},{10... | collective-permute-start | bytes 1966088 | tf_op jit(solution)/shard_map/ppermute | solution.py:112
  190.1 23.3 %copy-start.30 = (bf16[2560,1024]{1,0:T(8,128)(2,1)}, bf16[2560,1024]{1,0:T(8,128)(2,1)S(1)}, u32[]{:S(2)}) copy-start(bf16[2560,1024]{1,0:T(8,128)(2,1)S(1)} %constant_dynamic-update-slice_fusion) | copy-start | bytes 15728644
  343.7 34.2 %copy-start.44 = (s32[256]{0:T(256)S(1)}, s32[256]{0:T(256)}, u32[]{:S(2)}) copy-start(s32[256]{0:T(256)} %copy-done.43) | copy-start | bytes 3076
  343.8 34.2 %copy-start.51 = (f32[256,1]{0,1:T(1,128)S(1)}, f32[256,1]{0,1:T(1,128)}, u32[]{:S(2)}) copy-start(f32[256,1]{0,1:T(1,128)} %get-tuple-element.105) | copy-start | bytes 3076
  343.8 37.3 %copy-start.42 = (s32[256]{0:T(256)S(1)}, s32[256]{0:T(256)}, u32[]{:S(2)}) copy-start(s32[256]{0:T(256)} %copy-done.41) | copy-start | bytes 3076
  343.8 37.3 %copy-start.50 = (f32[256,1]{0,1:T(1,128)S(1)}, f32[256,1]{0,1:T(1,128)}, u32[]{:S(2)}) copy-start(f32[256,1]{0,1:T(1,128)} %get-tuple-element.104) | copy-start | bytes 3076
  343.8 40.5 %copy-start.38 = (f32[1024]{0:T(1024)S(1)}, f32[1024]{0:T(1024)}, u32[]{:S(2)}) copy-start(f32[1024]{0:T(1024)} %param.18) | copy-start | bytes 12292
  343.8 40.5 %copy-start.40 = (f32[256]{0:T(256)S(1)}, f32[256]{0:T(256)}, u32[]{:S(2)}) copy-start(f32[256]{0:T(256)} %copy-done.39) | copy-start | bytes 3076
  344.9 58.0 %collective-permute-start.5 = (bf16[256,2048]{0,1:T(8,128)(2,1)}, bf16[256,2048]{0,1:T(8,128)(2,1)}, u32[]{:S(2)}, u32[]{:S(2)}) collective-permute-start(bf16[256,2048]{0,1:T(8,128)(2,1)} %fusion.59), channel_id=1, source_target_pairs={{0,4},{4,0},{1,5},{5,1},{2,6},{6,2},{3,7},{7,3},{8,12},{12,8},{9,1... | collective-permute-start | bytes 3145736 | tf_op jit(solution)/shard_map/ppermute | solution.py:420
  393.7 88.9 %collective-permute-start.8 = (bf16[320,1152]{1,0:T(8,128)(2,1)}, bf16[320,1152]{1,0:T(8,128)(2,1)S(1)}, u32[]{:S(2)}, u32[]{:S(2)}) collective-permute-start(bf16[320,1152]{1,0:T(8,128)(2,1)} %slice.153), channel_id=1, source_target_pairs={{0,16},{8,24},{16,0},{24,8},{1,17},{9,25},{17,1},{25,9},{2,18},{10... | collective-permute-start | bytes 2211848 | tf_op jit(solution)/shard_map/ppermute | solution.py:111
  396.2 87.3 %collective-permute-start.9 = (bf16[320,1152]{1,0:T(8,128)(2,1)}, bf16[320,1152]{1,0:T(8,128)(2,1)}, u32[]{:S(2)}, u32[]{:S(2)}) collective-permute-start(bf16[320,1152]{1,0:T(8,128)(2,1)} %slice.154), channel_id=1, source_target_pairs={{0,8},{8,0},{16,24},{24,16},{1,9},{9,1},{17,25},{25,17},{2,10},{10... | collective-permute-start | bytes 2211848 | tf_op jit(solution)/shard_map/ppermute | solution.py:112
  411.8 65.1 %copy-start.46 = (f32[256]{0:T(256)S(1)}, f32[256]{0:T(256)}, u32[]{:S(2)}) copy-start(f32[256]{0:T(256)} %copy-done.45) | copy-start | bytes 3076
  411.8 69.5 %copy-start.9 = (f32[256,1024]{1,0:T(8,128)S(1)}, f32[256,1024]{1,0:T(8,128)}, u32[]{:S(2)}) copy-start(f32[256,1024]{1,0:T(8,128)} %copy-done.7) | copy-start | bytes 3145732
  412.9 68.4 %copy-start.28 = (f32[256,1024]{1,0:T(8,128)S(1)}, f32[256,1024]{1,0:T(8,128)}, u32[]{:S(2)}) copy-start(f32[256,1024]{1,0:T(8,128)} %get-tuple-element.117) | copy-start | bytes 3145732
  514.7 22.5 %copy-start.10 = (bf16[2560,1152]{1,0:T(8,128)(2,1)S(1)}, bf16[2560,1152]{1,0:T(8,128)(2,1)}, u32[]{:S(2)}) copy-start(bf16[2560,1152]{1,0:T(8,128)(2,1)} %constant_dynamic-update-slice_fusion.5) | copy-start | bytes 17694724
  599.2 17.7 %copy-start.33 = (f32[32,1024]{1,0:T(8,128)S(1)}, f32[32,1024]{1,0:T(8,128)}, u32[]{:S(2)}) copy-start(f32[32,1024]{1,0:T(8,128)} %get-tuple-element.140) | copy-start | bytes 393220
  599.3 18.3 %copy-start.32 = (f32[32,1024]{1,0:T(8,128)S(1)}, f32[32,1024]{1,0:T(8,128)}, u32[]{:S(2)}) copy-start(f32[32,1024]{1,0:T(8,128)} %get-tuple-element.141) | copy-start | bytes 393220
  599.3 19.0 %copy-start.1 = (bf16[1024,1024]{1,0:T(8,128)(2,1)S(1)}, bf16[1024,1024]{1,0:T(8,128)(2,1)}, u32[]{:S(2)}) copy-start(bf16[1024,1024]{1,0:T(8,128)(2,1)} %param.21) | copy-start | bytes 6291460
  (36 other events, 296.8 us)

commit v2 on v1

--- a/solution.py
+++ b/solution.py
@@ -65,20 +65,37 @@
     )
 
 
+def flipped(index, mask, size):
+    bit = 1
+    while bit < size:
+        if mask & bit:
+            index = index + bit * (1 - 2 * lax.rem(lax.div(index, bit), 2))
+        bit *= 2
+    return index
+
+
+def partners(n_row, n_col):
+    row, col = lax.axis_index("erow"), lax.axis_index("ecol")
+    return [
+        {"erow": flipped(row, place % n_row, n_row), "ecol": flipped(col, place // n_row, n_col)}
+        for place in range(n_row * n_col)
+    ]
+
+
 def exchange_kernel(sizes, blocks, landed, send_sems, recv_sems, own_sem):
-    rows, columns = sizes
-    group = rows * columns
-    me = lax.axis_index("erow") * columns + lax.axis_index("ecol")
-    peers = []
-    for shift in range(1, group):
-        peer = lax.rem(me + shift, group)
-        peers.append((peer, {"erow": lax.div(peer, columns), "ecol": lax.rem(peer, columns)}))
-    greet([device for _, device in peers])
-    own = pltpu.make_async_copy(blocks.at[me], landed.at[me], own_sem)
+    devices = partners(*sizes)
+    greet(devices[1:])
+    own = pltpu.make_async_copy(blocks.at[0], landed.at[0], own_sem)
     own.start()
     copies = []
-    for at, (peer, device) in enumerate(peers):
-        copy = remote(blocks.at[peer], landed.at[me], send_sems.at[at], recv_sems.at[at], device)
+    for place in range(1, len(devices)):
+        copy = remote(
+            blocks.at[place],
+            landed.at[place],
+            send_sems.at[place - 1],
+            recv_sems.at[place - 1],
+            devices[place],
+        )
         copy.start()
         copies.append(copy)
     for copy in copies:
@@ -228,6 +245,218 @@
     )(*shaped)
 
 
+def iota(shape, dimension):
+    return lax.broadcasted_iota(jnp.int32, shape, dimension)
+
+
+def row_slots(routes, live, experts, room, capacity):
+    tok = live.shape[1]
+    names = iota((experts, tok), 0)
+    hot = [(routes[k : k + 1] == names) & live for k in range(2)]
+    both = jnp.where(hot[0] | hot[1], 1.0, 0.0).astype(jnp.bfloat16)
+    before = jnp.where(iota((tok, tok), 0) < iota((tok, tok), 1), 1.0, 0.0).astype(jnp.bfloat16)
+    earlier = product(both, before)
+    slots = []
+    for k in range(2):
+        place = jnp.sum(jnp.where(hot[k], earlier, 0.0), axis=0, keepdims=True)
+        slot = routes[k : k + 1].astype(jnp.float32) * room + place
+        slots.append(jnp.where(live & (place < capacity), slot, -1.0))
+    return slots
+
+
+def bias_tables(relative_bias, table_width, offset):
+    buckets = relative_bias.shape[1]
+    place = iota((buckets, table_width), 1)
+    distance = jnp.where(place < table_width // 2, place, place - table_width) + offset
+    hot = jnp.where(bucket_of(distance) == iota((buckets, table_width), 0), 1.0, 0.0)
+    return jnp.dot(relative_bias, hot, precision=highest, preferred_element_type=jnp.float32)
+
+
+def skewed(row, rows):
+    width = row.shape[1]
+    full = pltpu.roll(jnp.broadcast_to(row, (rows, width)), 0, 1, stride=1, stride_axis=0)
+    return full[:, : width // 2]
+
+
+def front_kernel(
+    dims,
+    lengths,
+    tokens,
+    cotangent,
+    routes_row,
+    routes_col,
+    attn_gain,
+    moe_gain,
+    relative_bias,
+    router,
+    query_weight,
+    key_weight,
+    value_weight,
+    out_weight,
+    normed_out,
+    query_out,
+    both_out,
+    probs_out,
+    mixed_out,
+    residual_out,
+    gates_out,
+    rows_out,
+    cot_landed,
+    select,
+    cot_slots,
+    tables,
+    held_weights,
+    weight_sems,
+    own_sem,
+    send_sems,
+    recv_sems,
+    row_send,
+    row_recv,
+):
+    heads, experts, room, capacity, n_row, n_col = dims
+    tok, width = tokens.shape
+    pair_width = 2 * width // heads
+    loads = []
+    for at, source in enumerate((key_weight, value_weight, query_weight, out_weight)):
+        load = pltpu.make_async_copy(source, held_weights.at[at], weight_sems.at[at])
+        load.start()
+        loads.append(load)
+    devices = partners(n_row, n_col)
+    barrier = pltpu.get_barrier_semaphore()
+    for device in devices[1:]:
+        pl.semaphore_signal(barrier, 1, device_id=device, device_id_type=MESH)
+
+    piece = lax.axis_index("erow")
+    length = lengths[0]
+    live = iota((1, tok), 1) + piece * tok < length
+    slots = row_slots(routes_row[...], live, experts, room, capacity)
+    names = iota((experts * room, tok), 0).astype(jnp.float32)
+    hot = [jnp.where(names == slot, 1.0, 0.0).astype(jnp.bfloat16) for slot in slots]
+    select[...] = hot[0] + hot[1]
+    cot_slots[...] = product(select[...], cotangent[...]).astype(jnp.bfloat16).reshape(cot_slots.shape)
+    pl.semaphore_wait(barrier, len(devices) - 1)
+    own = pltpu.make_async_copy(cot_slots.at[0], cot_landed.at[0], own_sem)
+    own.start()
+    copies = []
+    for place in range(1, len(devices)):
+        copy = remote(
+            cot_slots.at[place],
+            cot_landed.at[place],
+            send_sems.at[place - 1],
+            recv_sems.at[place - 1],
+            devices[place],
+        )
+        copy.start()
+        copies.append(copy)
+
+    inputs = tokens[...].astype(jnp.float32)
+    scale = lax.rsqrt(jnp.mean(inputs * inputs, axis=1, keepdims=True) + epsilon)
+    normed = (inputs * scale * attn_gain[...]).astype(jnp.bfloat16)
+    normed_out[...] = normed
+    loads[0].wait()
+    both_out[:tok, :width] = product(normed, held_weights[0]).astype(jnp.bfloat16)
+    loads[1].wait()
+    both_out[:tok, width:] = product(normed, held_weights[1]).astype(jnp.bfloat16)
+    pair_copy = remote(both_out.at[pl.ds(0, tok)], both_out.at[pl.ds(tok, tok)], row_send, row_recv, devices[1])
+    pair_copy.start()
+    loads[2].wait()
+    query_out[...] = (product(normed, held_weights[2]) * 0.125).astype(jnp.bfloat16)
+    offset = tok * (1 - 2 * piece)
+    tables[:, : 2 * tok] = bias_tables(relative_bias[...], 2 * tok, 0)
+    tables[:, 2 * tok :] = bias_tables(relative_bias[...], 2 * tok, offset)
+    place = iota((1, 2 * tok), 1)
+    position = jnp.where(place < tok, place + piece * tok, place - tok + (1 - piece) * tok)
+    dead = jnp.where(position < length, 0.0, -1000000000.0)
+    low_half = iota((tok, pair_width), 1) < pair_width // 2
+    pair_copy.wait()
+
+    def attend(pair, carry):
+        lanes = pl.ds(pl.multiple_of(pair * pair_width, pair_width), pair_width)
+        value_lanes = pl.ds(pl.multiple_of(width + pair * pair_width, pair_width), pair_width)
+        queries, keys, values = query_out[:, lanes], both_out[:, lanes], both_out[:, value_lanes]
+        results = []
+        for member in range(2):
+            mask = low_half if member == 0 else jnp.logical_not(low_half)
+            head = 2 * pair + member
+            scores = product_back(jnp.where(mask, queries, jnp.zeros_like(queries)), keys)
+            table = tables[pl.ds(head, 1)]
+            bias = jnp.concatenate([skewed(table[:, : 2 * tok], tok), skewed(table[:, 2 * tok :], tok)], axis=1)
+            scores = scores + bias + dead
+            powers = jnp.exp(scores - jnp.max(scores, axis=1, keepdims=True))
+            probs = (powers * (1.0 / jnp.sum(powers, axis=1, keepdims=True))).astype(jnp.bfloat16)
+            probs_out[pl.ds(head, 1)] = probs[None]
+            results.append(product(probs, values))
+        mixed_out[:, lanes] = jnp.where(low_half, results[0], results[1]).astype(jnp.bfloat16)
+        return carry
+
+    lax.fori_loop(0, heads // 2, attend, 0)
+    loads[3].wait()
+    residual = inputs + product(mixed_out[...], held_weights[3])
+    residual_out[...] = residual
+    scale = lax.rsqrt(jnp.mean(residual * residual, axis=1, keepdims=True) + epsilon)
+    moe_in = residual * scale * moe_gain[...]
+    logits = jnp.dot(moe_in, router[...], precision=highest, preferred_element_type=jnp.float32)
+    lane = iota(logits.shape, 1)
+    logits = jnp.where(lane < experts, logits, -1e30)
+    powers = jnp.exp(logits - jnp.max(logits, axis=1, keepdims=True))
+    gates = powers / jnp.sum(powers, axis=1, keepdims=True)
+    gates_out[...] = gates
+    panel = jnp.zeros((experts * room, LANES), jnp.float32)
+    for k in range(2):
+        pick = jnp.sum(jnp.where(routes_col[:, k : k + 1] == lane, gates, 0.0), axis=1, keepdims=True)
+        high = pick.astype(jnp.bfloat16)
+        low = (pick - high.astype(jnp.float32)).astype(jnp.bfloat16)
+        parts = jnp.where(lane == 0, high, jnp.where(lane == 1, low, jnp.zeros_like(low)))
+        panel = panel + product(hot[k], parts)
+    rows = product(select[...], moe_in.astype(jnp.bfloat16))
+    rows_out[:, :, :width] = rows.astype(jnp.bfloat16).reshape(rows_out.shape[0], -1, width)
+    rows_out[:, :, width:] = panel.astype(jnp.bfloat16).reshape(rows_out.shape[0], -1, LANES)
+    for copy in copies:
+        copy.wait()
+    own.wait()
+
+
+def front(dims, number, lengths, tokens, cotangent, routes_row, routes_col, *params):
+    heads, experts, room, capacity, n_row, n_col = dims
+    tok, width = tokens.shape
+    group = n_row * n_col
+    blocks = experts * room // group
+    half, single = jnp.bfloat16, jnp.float32
+    vmem, anywhere = pl.BlockSpec(memory_space=pltpu.VMEM), pl.BlockSpec(memory_space=pl.ANY)
+    shapes = [
+        ((tok, width), half),
+        ((tok, width), half),
+        ((2 * tok, 2 * width), half),
+        ((heads, tok, 2 * tok), half),
+        ((tok, width), half),
+        ((tok, width), single),
+        ((tok, LANES), single),
+        ((group, blocks, width + LANES), half),
+        ((group, blocks, width), half),
+    ]
+    return pl.pallas_call(
+        functools.partial(front_kernel, dims),
+        out_shape=[jax.ShapeDtypeStruct(shape, kind) for shape, kind in shapes],
+        in_specs=[pl.BlockSpec(memory_space=pltpu.SMEM)] + [vmem] * 8 + [anywhere] * 4,
+        out_specs=[vmem] * 8 + [anywhere],
+        scratch_shapes=[
+            pltpu.VMEM((experts * room, tok), half),
+            pltpu.VMEM((group, blocks, width), half),
+            pltpu.VMEM((heads, 4 * tok), single),
+            pltpu.VMEM((4, width, width), half),
+            pltpu.SemaphoreType.DMA((4,)),
+            pltpu.SemaphoreType.DMA,
+            pltpu.SemaphoreType.DMA((group - 1,)),
+            pltpu.SemaphoreType.DMA((group - 1,)),
+            pltpu.SemaphoreType.DMA,
+            pltpu.SemaphoreType.DMA,
+        ],
+        compiler_params=pltpu.CompilerParams(
+            collective_id=number, has_side_effects=True, vmem_limit_bytes=VMEM_LIMIT
+        ),
+    )(lengths, tokens, cotangent, routes_row, routes_col, *params)
+
+
 def gelu_parts(gate_part):
     inner = 0.7978845608028654 * (gate_part + 0.044715 * gate_part * gate_part * gate_part)
     bend = jnp.tanh(inner)
@@ -300,13 +529,12 @@
     bias_onehot = (
         jnp.arange(bucket_count, dtype=jnp.int32)[:, None, None] == bucket_ids[None]
     ).astype(jnp.bfloat16)
-    bias_full = jnp.einsum(
-        "zt,tyx->zyx", relative_bias, bias_onehot, precision=highest, preferred_element_type=jnp.float32
-    )
-    key_live = key_pos < seq_length
     tok_live = query_pos < seq_length
     pair_routes = routes[0]
-    route_flat = pair_routes.reshape(-1)
+    near_routes = (
+        (pair_routes % n_col) ^ lax.axis_index("ecol")
+    ) * n_row + ((pair_routes // n_col) ^ piece)
+    route_flat = near_routes.reshape(-1)
     pair_live = jnp.broadcast_to(tok_live[:, None], pair_routes.shape).reshape(-1)
     expert_range = jnp.arange(expert_count, dtype=jnp.int32)
     route_hot = ((route_flat[:, None] == expert_range[None, :]) & pair_live[:, None]).astype(jnp.int32)
@@ -325,47 +553,47 @@
             rows.shape
         )
 
-    out_grad_low = cotangent[0]
-    out_grad = out_grad_low.astype(jnp.float32)
-    got_grads = sent(rounded(product_left(select_both, out_grad_low)), 0)
+    out_grad = cotangent[0].astype(jnp.float32)
+    routes_row = jnp.pad(near_routes.T, ((0, 6), (0, 0)))
+    (
+        normed,
+        queries,
+        both_all,
+        probs_low,
+        mixed,
+        residual,
+        gates,
+        slot_rows,
+        got_grads,
+    ) = front(
+        (head_count, expert_count, room, capacity, n_row, n_col),
+        0,
+        lengths,
+        tokens[0],
+        cotangent[0],
+        routes_row,
+        pair_routes,
+        attn_gain[None],
+        moe_gain[None],
+        relative_bias,
+        jnp.pad(router_weight, ((0, 0), (0, LANES - expert_count))),
+        query_weight,
+        key_weight,
+        value_weight,
+        out_weight,
+    )
+    got_grads = got_grads.reshape(slot_count, width)
     all_grads = replicas(got_grads)
     down_rows = product_back(all_grads, down_mat)
-
-    normed = rounded(rms_scale(inputs, attn_gain))
-    queries = rounded(product(normed, query_weight))
-    both_local = jnp.concatenate(
-        [rounded(product(normed, key_weight)), rounded(product(normed, value_weight))], axis=1
-    )
-    both_other = lax.ppermute(both_local, "erow", [(0, 1), (1, 0)])
-    both_all = jnp.concatenate([both_local, both_other], axis=0)
     seq_rows = both_all.shape[0]
     query_heads = queries.reshape(tok_rows, head_count, head_size)
     key_heads = both_all[:, :width].reshape(seq_rows, head_count, head_size)
     value_heads = both_all[:, width:].reshape(seq_rows, head_count, head_size)
-    scores = (
-        jnp.einsum("qhd,khd->hqk", query_heads, key_heads, preferred_element_type=jnp.float32) * 0.125
-        + bias_full
-    )
-    scores = jnp.where(key_live[None, None, :], scores, -1000000000.0)
-    attn_probs = jax.nn.softmax(scores, axis=-1)
-    probs_low = rounded(attn_probs)
-    mixed = rounded(
-        jnp.einsum("hqk,khd->qhd", probs_low, value_heads, preferred_element_type=jnp.float32).reshape(
-            tok_rows, width
-        )
-    )
-    residual = inputs + product(mixed, out_weight)
+    attn_probs = probs_low.astype(jnp.float32)
+    gate_probs = gates[:, :expert_count]
+    gate_pick = jnp.sum(gate_probs[:, None, :] * choice_hot, axis=-1)
     moe_in = rms_scale(residual, moe_gain)
-    gate_probs = jax.nn.softmax(jnp.dot(moe_in, router_weight, precision=highest), axis=-1)
-    gate_pick = jnp.sum(gate_probs[:, None, :] * choice_hot, axis=-1)
-
-    slot_pick = lax.dot_general(
-        select_lead.astype(jnp.float32), gate_pick[:, 0:1], (((0,), (0,)), ((), ())), precision=highest
-    ) + lax.dot_general(
-        select_trail.astype(jnp.float32), gate_pick[:, 1:2], (((0,), (0,)), ((), ())), precision=highest
-    )
-    slot_rows = rounded(product_left(select_both, rounded(moe_in)))
-    got = sent(jnp.concatenate([slot_rows, split_scalar(slot_pick)], axis=1), 1)
+    got = sent(slot_rows.reshape(slot_count, -1), 1)
     all_got = replicas(got)
     own_rows, own_picks = got[:, :width], join_scalar(got[:, width:])
     hidden, gate_back, up_back = expert_parts(
@@ -411,7 +639,7 @@
         jnp.einsum("hqk,khd->qhd", score_back, key_heads, preferred_element_type=jnp.float32) * 0.125
     ).reshape(tok_rows, width)
     key_part = (
-        jnp.einsum("hqk,qhd->khd", score_back, query_heads, preferred_element_type=jnp.float32) * 0.125
+        jnp.einsum("hqk,qhd->khd", score_back, query_heads, preferred_element_type=jnp.float32)
     ).reshape(seq_rows, width)
     value_part = jnp.einsum(
         "hqk,qhd->khd", probs_low, mixed_grad, preferred_element_type=jnp.float32

time: 626 us -> 569 us (0.909)
  matrix products: 306 us -> 240 us
  other arithmetic: 23.6 us -> 13.3 us
  waiting for transfers between devices: 25.2 us -> 35.2 us
  local copies, waits for them, and re-layouts: 51.3 us -> 58.6 us
    pallas_call x4 -> x3, Pallas kernels: 136 us -> 102 us  [exchange(): pl.pallas_call(functools.partial(exchange_kernel, sizes), out_shape=jax.S...]
    dot_general x6 -> x0, matrix products: 33.1 us -> none  [the longest x1 14.5 us: body(): jnp.einsum('hqk,khd->qhd', probs_low, value_heads, preferred_element_type...]
    pallas_call x0 -> x1, Pallas kernels: none -> 32.6 us  [front(): pl.pallas_call(functools.partial(front_kernel, dims), out_shape=[jax.Shap...]
    ppermute x2, waiting for transfers between devices: 0.01 us -> 32.3 us  [replicas(): by_first = lax.ppermute(block, 'dp', first)]
    ppermute x2, waiting for transfers between devices: 25.1 us -> 0.15 us  [replicas(): upper = lax.ppermute(by_first[:half], 'dp', second)]
    dot_general x1, matrix products: 14.8 us -> 3.18 us  [body(): jnp.einsum('hqk,qhd->khd', probs_low, mixed_grad, preferred_element_type=...]
    dot_general x12 -> x8, matrix products: 98.7 us -> 91.2 us  [product(): return jnp.dot(left_side, right_side, preferred_element_type=jnp.float32)]
    dot_general x9 -> x7, matrix products: 88 us -> 83.2 us  [product_left(): lax.dot_general(left_side, right_side, (((0,), (0,)), ((), ())), preferre...]
  transfers between devices with their start and end apart: 10 -> 9, of which waited for: 1 -> 3; matrix products, arithmetic and copies ran while one was open for 38% -> 50% of each run, Pallas kernels for 27% -> 12%
where the time goes in v2:
time: 569 us; the launch traced here: 559 us
  matrix products  240 us (42%)
  Pallas kernels  201 us (35%)
  local copies, waits for them, and re-layouts  58.6 us (10%)
  waiting for transfers between devices  35.2 us (6%)
  other arithmetic  13.3 us (2%)
  starting transfers between devices  8.6 us (2%)
    pallas_call x3, Pallas kernels, exchange(): pl.pallas_call(functools.partial(exchange_kernel, sizes), out_shape=jax.S...  102 us
    dot_general x8, matrix products, product(): return jnp.dot(left_side, right_side, preferred_element_type=jnp.float32)  91.2 us
    dot_general x7, matrix products, product_left(): lax.dot_general(left_side, right_side, (((0,), (0,)), ((), ())), preferre...  83.2 us
    pallas_call x1, Pallas kernels, reduce_shares(): pl.pallas_call(functools.partial(reduce_kernel, (n_dp, n_row, n_col, dept...  66.6 us
    dot_general x7, matrix products, product_back(): lax.dot_general(left_side, right_side, (((1,), (1,)), ((), ())), preferre...  50.7 us
    pallas_call x1, Pallas kernels, front(): pl.pallas_call(functools.partial(front_kernel, dims), out_shape=[jax.Shap...  32.6 us
    ppermute x2, waiting for transfers between devices, replicas(): by_first = lax.ppermute(block, 'dp', first)  32.3 us
    unnamed x99, local copies, waits for them, and re-layouts  26.5 us
  transfers between devices with their start and end apart: 9, of which 3 were waited for; matrix products, arithmetic and copies ran while one was open for 50% of the time, Pallas kernels for 12%

profile of v2, /device:TPU:0, one launch (start us, length us, event | category | flops | bytes accessed | tf_op | source)
XLA Modules:
  0.0 559.4 jit_solution(18393957286424591658)
XLA Ops:
  7.3 32.6 %shard_map.246 = (bf16[256,1024]{1,0:T(8,128)(2,1)}, bf16[256,1024]{1,0:T(8,128)(2,1)}, bf16[512,2048]{1,0:T(8,128)(2,1)}, bf16[16,256,512]{2,1,0:T(8,128)(2,1)}...) custom-call(s32[1]{0:T(128)} %copy.136.lengths, ...), custom_call_target="tpu_custom_call" | custom-call | tf_op jit(solution)/shard_map/pallas_call | solution.py:437
  40.0 35.1 %shard_map.247 = bf16[8,80,1152]{2,1,0:T(8,128)(2,1)} custom-call(bf16[8,80,1152]{2,1,0:T(8,128)(2,1)} %get-tuple-element.29.blocks), custom_call_target="tpu_custom_call" | custom-call | tf_op jit(solution)/shard_map/pallas_call | solution.py:108
  79.3 2.5 constant_dynamic-update-slice_fusion.4
  83.4 3.0 fusion.176
  86.4 2.3 copy.111
  90.7 2.3 copy.109
  96.4 9.3 %fusion.38 = f32[640,2816]{1,0:T(8,128)} fusion(bf16[1,1024,2816]{2,1,0:T(8,128)(2,1)} %param.26, bf16[640,1152]{1,0:T(8,128)(2,1)S(1)} %bitcast.139), kind=kOutput, calls=%fused_computation.51 | convolution fusion | flops 3690987520 | bytes 14286848 | tf_op jit(solution)/shard_map/dot_general | solution.py:35
  105.8 32.3 %collective-permute-done = bf16[640,1024]{1,0:T(8,128)(2,1)} collective-permute-done((bf16[640,1024]{1,0:T(8,128)(2,1)}, bf16[640,1024]{1,0:T(8,128)(2,1)}, u32[]{:S(2)}, u32[]{:S(2)}) %collective-permute-start) | collective-permute-done | bytes 1310752 | tf_op jit(solution)/shard_map/ppermute | solution.py:126
  146.4 2.2 slice.153
  151.6 2.6 constant_dynamic-update-slice_fusion.8
  154.2 2.6 constant_dynamic-update-slice_fusion.7
  157.0 2.7 collective-permute-done.3
  159.8 18.7 %fusion.24 = f32[2560,2816]{1,0:T(8,128)} fusion(bf16[2560,1024]{1,0:T(8,128)(2,1)S(1)} %constant_dynamic-update-slice_fusion, bf16[1,2816,1024]{2,1,0:T(8,128)(2,1)S(1)} %bitcast.170), kind=kOutput, calls=%fused_computation.37 | convolution fusion | flops 14763950080 | bytes 39845888 | tf_op jit(solution)/shard_map/dot_general | solution.py:39
  178.5 11.1 %multiply_reduce_fusion = (f32[640]{0:T(1024)S(1)}, f32[640,2816]{1,0:T(8,128)}) fusion(f32[2560,2816]{1,0:T(8,128)} %fusion.24, f32[640,2816]{1,0:T(8,128)} %fusion.38, bf16[1,1024,2816]{2,1,0:T(8,128)(2,1)} %param.27, bf16[640,1152]{1,0:T(8,128)(2,1)S(1)} %bitcast.140), kind=kOutput, calls=%fused_computation.33 | convolution fusion | flops 3710811648 | bytes 28707328 | tf_op jit(solution)/shard_map/dot_general | solution.py:35
  189.6 10.8 %fusion.30 = f32[640,1024]{1,0:T(8,128)} fusion(bf16[1,1024,2816]{2,1,0:T(8,128)(2,1)} %param.27, f32[2560,2816]{1,0:T(8,128)} %fusion.24, f32[640]{0:T(1024)S(1)} %add_reduce_fusion.1, f32[640,2816]{1,0:T(8,128)} %fusion.38), kind=kOutput, calls=%fused_computation.43 | convolution fusion | flops 3710812160 | bytes 22809088 | tf_op jit(solution)/shard_map/dot_general | solution.py:39
  200.6 15.0 %add_convert_fusion = bf16[640,1024]{1,0:T(8,128)(2,1)S(1)} fusion(f32[640,1024]{1,0:T(8,128)} %fusion.30, bf16[1,1024,2816]{2,1,0:T(8,128)(2,1)} %param.26, f32[640,2816]{1,0:T(8,128)} %fusion.38, f32[640,2816]{1,0:T(8,128)} %get-tuple-element.127, f32[2560,2816]{1,0:T(8,128)} %fusion.24, f32[640]{0:T(1024)S(1)} %add_reduce_fusion.1), kind=kOutput, calls=%fused_computation.65 | convolution fusion | flops 3730145280 | bytes 31328768 | tf_op jit(solution)/shard_map/dot_general | solution.py:39
  216.9 34.7 %shard_map.249 = bf16[8,80,1152]{2,1,0:T(8,128)(2,1)} custom-call(bf16[8,80,1152]{2,1,0:T(8,128)(2,1)} %bitcast.141), custom_call_target="tpu_custom_call" | custom-call | tf_op jit(solution)/shard_map/pallas_call | solution.py:108
  255.9 12.5 %fusion.64 = bf16[640,1024]{1,0:T(8,128)(2,1)} fusion(bf16[1,2816,1024]{2,1,0:T(8,128)(2,1)} %param.28, f32[640,2816]{1,0:T(8,128)} %get-tuple-element.127, f32[640,2816]{1,0:T(8,128)} %fusion.38), kind=kOutput, calls=%fused_computation.80 | convolution fusion | flops 3709665280 | bytes 21495808 | tf_op jit(solution)/shard_map/dot_general | solution.py:35
  271.1 2.7 convolution_convert_fusion.4
  274.0 3.2 fusion.181
  286.7 4.2 fusion.81
  291.6 2.1 convolution_convert_fusion.2
  293.7 32.0 %shard_map.248 = bf16[8,80,1024]{2,1,0:T(8,128)(2,1)} custom-call(bf16[8,80,1024]{2,1,0:T(8,128)(2,1)} %bitcast.160), custom_call_target="tpu_custom_call" | custom-call | tf_op jit(solution)/shard_map/pallas_call | solution.py:108
  327.7 2.7 fusion.76
  338.1 29.1 %multiply_multiply_fusion.1 = (f32[2560,2816]{1,0:T(8,128)}, f32[2560,2816]{1,0:T(8,128)}) fusion(bf16[1,1024,2816]{2,1,0:T(8,128)(2,1)} %param.26, bf16[2560,1152]{1,0:T(8,128)(2,1)} %constant_dynamic-update-slice_fusion.5), kind=kOutput, calls=%fused_computation.10 | convolution fusion | flops 14821621760 | bytes 68681728 | tf_op jit(solution)/shard_map/dot_general | solution.py:35
  367.2 22.4 %fusion.28 = f32[2560,2816]{1,0:T(8,128)} fusion(bf16[1,1024,2816]{2,1,0:T(8,128)(2,1)} %param.27, bf16[2560,1152]{1,0:T(8,128)(2,1)} %constant_dynamic-update-slice_fusion.5), kind=kOutput, calls=%fused_computation.41 | convolution fusion | flops 14763950080 | bytes 39845888 | tf_op jit(solution)/shard_map/dot_general | solution.py:35
  391.5 3.1 slice.155
  394.6 2.3 copy-done.11
  396.9 23.7 %fusion.41 = f32[1,256,2816]{2,1,0:T(8,128)} fusion(f32[2560,2816]{1,0:T(8,128)} %fusion.24, f32[2560]{0:T(1024)S(1)} %add_reduce_fusion, bf16[2560,1024]{1,0:T(8,128)(2,1)S(1)} %slice.155, s32[]{:T(128)S(6)} %select_n.70, f32[2560,2816]{1,0:T(8,128)} %get-tuple-element.133), kind=kOutput, calls=%fused_computation.56 | convolution fusion | flops 3770286080 | bytes 61878276 | tf_op jit(solution)/shard_map/dot_general | solution.py:45
  420.6 34.6 %fusion.42 = f32[1,256,2816]{2,1,0:T(8,128)} fusion(f32[2560,2816]{1,0:T(8,128)} %get-tuple-element.133, f32[2560,2816]{1,0:T(8,128)} %fusion.28, f32[2560,2816]{1,0:T(8,128)} %fusion.24, f32[2560]{0:T(1024)S(1)} %add_reduce_fusion, bf16[2560,1024]{1,0:T(8,128)(2,1)} %copy-done.11, s32[]{:T(128)S(6)} %select_n.70), kind=kOutput, calls=%fused_computation.57 | convolution fusion | flops 3842375680 | bytes 90712064 | tf_op jit(solution)/shard_map/dot_general | solution.py:45
  455.3 16.4 %fusion.57 = f32[1,704,1024]{2,1,0:T(8,128)} fusion(bf16[2560,1024]{1,0:T(8,128)(2,1)} %copy-done.26, f32[2560,2816]{1,0:T(8,128)} %fusion.28, s32[]{:T(128)S(6)} %select_n.71, f32[2560,2816]{1,0:T(8,128)} %get-tuple-element.132, f32[2560]{0:T(1024)S(1)} %add_reduce_fusion), kind=kOutput, calls=%fused_computation.79 | convolution fusion | flops 3696394240 | bytes 23865348 | tf_op jit(solution)/shard_map/dot_general | solution.py:45
  480.7 66.6 %shard_map.250 = (f32[32,1024]{1,0:T(8,128)}, f32[32,1024]{1,0:T(8,128)}, f32[32,1024]{1,0:T(8,128)}, f32[32,1024]{1,0:T(8,128)}, f32[32,128]{1,0:T(8,128)}) custom-call(bf16[2,2,2,128,1024]{4,3,2,1,0:T(8,128)(2,1)} %bitcast.131, bf16[2,2,2,128,1024]{4,3,2,1,0:T(8,128)(2,1)} %bitcast.132, bf16[2,2,2,128,1024]{4,3,2,1,0:T(8,128)(2,1)} %bitcast.134, ...), custom_call_target="tpu_custom_call" | custom-call | tf_op jit(solution)/shard_map/pallas_call | solution.py:236
  (194 shorter events, 79.6 us)
Async XLA Ops:
  1.5 5.9 %copy-start.12 = (s32[1,256,2]{2,1,0:T(8,128)}, s32[1,256,2]{2,1,0:T(8,128)S(1)}, u32[]{:S(2)}) copy-start(s32[1,256,2]{2,1,0:T(8,128)S(1)} %copy.97) | copy-start | bytes 6148
  7.3 75.4 %copy-start.13 = (bf16[1,256,1024]{2,1,0:T(8,128)(2,1)S(1)}, bf16[1,256,1024]{2,1,0:T(8,128)(2,1)}, u32[]{:S(2)}) copy-start(bf16[1,256,1024]{2,1,0:T(8,128)(2,1)} %param.15) | copy-start | bytes 1572868
  40.0 43.2 %copy-start.20 = (f32[256,128]{1,0:T(8,128)S(1)}, f32[256,128]{1,0:T(8,128)}, u32[]{:S(2)}) copy-start(f32[256,128]{1,0:T(8,128)} %get-tuple-element.28) | copy-start | bytes 393220
  40.0 43.2 %copy-start.1 = (f32[256,1024]{1,0:T(8,128)S(1)}, f32[256,1024]{1,0:T(8,128)}, u32[]{:S(2)}) copy-start(f32[256,1024]{1,0:T(8,128)} %get-tuple-element.27) | copy-start | bytes 3145732
  75.1 71.2 %collective-permute-start.5 = (bf16[640,1152]{1,0:T(8,128)(2,1)}, bf16[640,1152]{1,0:T(8,128)(2,1)}, u32[]{:S(2)}, u32[]{:S(2)}) collective-permute-start(bf16[640,1152]{1,0:T(8,128)(2,1)} %bitcast.135), channel_id=1, source_target_pairs={{0,8},{8,0},{16,24},{24,16},{1,9},{9,1},{17,25},{25,17},{2,10},{10... | collective-permute-start | bytes 4423688 | tf_op jit(solution)/shard_map/ppermute | solution.py:126
  76.7 72.4 %collective-permute-start.6 = (bf16[640,1152]{1,0:T(8,128)(2,1)}, bf16[640,1152]{1,0:T(8,128)(2,1)}, u32[]{:S(2)}, u32[]{:S(2)}) collective-permute-start(bf16[640,1152]{1,0:T(8,128)(2,1)} %bitcast.136), channel_id=1, source_target_pairs={{0,16},{8,24},{16,0},{24,8},{1,17},{9,25},{17,1},{25,9},{2,18},{10... | collective-permute-start | bytes 4423688 | tf_op jit(solution)/shard_map/ppermute | solution.py:127
  78.2 59.9 %collective-permute-start = (bf16[640,1024]{1,0:T(8,128)(2,1)}, bf16[640,1024]{1,0:T(8,128)(2,1)}, u32[]{:S(2)}, u32[]{:S(2)}) collective-permute-start(bf16[640,1024]{1,0:T(8,128)(2,1)} %bitcast.157), channel_id=1, source_target_pairs={{0,8},{8,0},{16,24},{24,16},{1,9},{9,1},{17,25},{25,17},{2,10},{10... | collective-permute-start | bytes 3932168 | tf_op jit(solution)/shard_map/ppermute | solution.py:126
  78.7 62.1 %collective-permute-start.1 = (bf16[640,1024]{1,0:T(8,128)(2,1)}, bf16[640,1024]{1,0:T(8,128)(2,1)}, u32[]{:S(2)}, u32[]{:S(2)}) collective-permute-start(bf16[640,1024]{1,0:T(8,128)(2,1)} %bitcast.158), channel_id=1, source_target_pairs={{0,16},{8,24},{16,0},{24,8},{1,17},{9,25},{17,1},{25,9},{2,18},{10... | collective-permute-start | bytes 3932168 | tf_op jit(solution)/shard_map/ppermute | solution.py:127
  82.7 12.2 %copy-start.10 = (bf16[8,80,1152]{2,1,0:T(8,128)(2,1)S(1)}, bf16[8,80,1152]{2,1,0:T(8,128)(2,1)}, u32[]{:S(2)}) copy-start(bf16[8,80,1152]{2,1,0:T(8,128)(2,1)} %shard_map.247) | copy-start | bytes 4423684
  82.9 12.3 %copy-start.33 = (f32[256]{0:T(256)}, f32[256]{0:T(256)S(1)}, u32[]{:S(2)}) copy-start(f32[256]{0:T(256)S(1)} %fusion.87) | copy-start | bytes 3076
  95.2 48.3 %slice-start = ((s8[5242880]{0:T(1024)(128)(4,1)}), s8[4194304]{0:T(1024)(128)(4,1)S(1)}, s32[]{:S(2)}) async-start(s8[5242880]{0:T(1024)(128)(4,1)} %bitcast.161), calls=%async_computation | async-start | bytes 8388608
  96.4 47.1 %slice-start.1 = ((s8[5242880]{0:T(1024)(128)(4,1)}), s8[1048576]{0:T(1024)(128)(4,1)S(1)}, s32[]{:S(2)}) async-start(s8[5242880]{0:T(1024)(128)(4,1)} %bitcast.161), calls=%async_computation.1 | async-start | bytes 2097152
  139.2 17.7 %collective-permute-start.2 = (bf16[320,1024]{1,0:T(8,128)(2,1)S(1)}, bf16[320,1024]{1,0:T(8,128)(2,1)S(1)}, u32[]{:S(2)}, u32[]{:S(2)}) collective-permute-start(bf16[320,1024]{1,0:T(8,128)(2,1)S(1)} %slice.143), channel_id=1, source_target_pairs={{0,16},{8,24},{16,0},{24,8},{1,17},{9,25},{17,1},{25,9},{2,18},{10... | collective-permute-start | bytes 1966088 | tf_op jit(solution)/shard_map/ppermute | solution.py:128
  142.0 17.7 %collective-permute-start.3 = (bf16[320,1024]{1,0:T(8,128)(2,1)S(1)}, bf16[320,1024]{1,0:T(8,128)(2,1)S(1)}, u32[]{:S(2)}, u32[]{:S(2)}) collective-permute-start(bf16[320,1024]{1,0:T(8,128)(2,1)S(1)} %slice.144), channel_id=1, source_target_pairs={{0,8},{8,0},{16,24},{24,16},{1,9},{9,1},{17,25},{25,17},{2,10},{10... | collective-permute-start | bytes 1966088 | tf_op jit(solution)/shard_map/ppermute | solution.py:129
  146.3 13.4 %slice-start.2 = ((s8[5767168]{0:T(1024)(128)(4,1)}), s8[4194304]{0:T(1024)(128)(4,1)S(1)}, s32[]{:S(2)}) async-start(s8[5767168]{0:T(1024)(128)(4,1)} %bitcast.169), calls=%async_computation.2 | async-start | bytes 8388608
  148.6 185.4 %collective-permute-start.7 = (bf16[320,1152]{1,0:T(8,128)(2,1)}, bf16[320,1152]{1,0:T(8,128)(2,1)}, u32[]{:S(2)}, u32[]{:S(2)}) collective-permute-start(bf16[320,1152]{1,0:T(8,128)(2,1)} %slice.153), channel_id=1, source_target_pairs={{0,16},{8,24},{16,0},{24,8},{1,17},{9,25},{17,1},{25,9},{2,18},{10... | collective-permute-start | bytes 2211848 | tf_op jit(solution)/shard_map/ppermute | solution.py:128
  151.1 8.6 %slice-start.3 = ((s8[5767168]{0:T(1024)(128)(4,1)}), s8[1572864]{0:T(1024)(128)(4,1)S(1)}, s32[]{:S(2)}) async-start(s8[5767168]{0:T(1024)(128)(4,1)} %bitcast.169), calls=%async_computation.3 | async-start | bytes 3145728
  151.1 184.9 %collective-permute-start.8 = (bf16[320,1152]{1,0:T(8,128)(2,1)}, bf16[320,1152]{1,0:T(8,128)(2,1)}, u32[]{:S(2)}, u32[]{:S(2)}) collective-permute-start(bf16[320,1152]{1,0:T(8,128)(2,1)} %slice.154), channel_id=1, source_target_pairs={{0,8},{8,0},{16,24},{24,16},{1,9},{9,1},{17,25},{25,17},{2,10},{10... | collective-permute-start | bytes 2211848 | tf_op jit(solution)/shard_map/ppermute | solution.py:129
  159.8 18.8 %copy-start.26 = (bf16[2560,1024]{1,0:T(8,128)(2,1)}, bf16[2560,1024]{1,0:T(8,128)(2,1)S(1)}, u32[]{:S(2)}) copy-start(bf16[2560,1024]{1,0:T(8,128)(2,1)S(1)} %constant_dynamic-update-slice_fusion) | copy-start | bytes 15728644
  255.9 13.0 %copy-start.27 = (f32[1024,8]{0,1:T(8,128)S(1)}, f32[1024,8]{0,1:T(8,128)}, u32[]{:S(2)}) copy-start(f32[1024,8]{0,1:T(8,128)} %param.25) | copy-start | bytes 98308
  255.9 13.0 %copy-start.29 = (f32[1024]{0:T(1024)S(1)}, f32[1024]{0:T(1024)}, u32[]{:S(2)}) copy-start(f32[1024]{0:T(1024)} %param.24) | copy-start | bytes 12292
  255.9 14.8 %copy-start.21 = (bf16[1,256,1024]{2,1,0:T(8,128)(2,1)S(1)}, bf16[1,256,1024]{2,1,0:T(8,128)(2,1)}, u32[]{:S(2)}) copy-start(bf16[1,256,1024]{2,1,0:T(8,128)(2,1)} %param.29) | copy-start | bytes 1572868
  271.1 60.8 %copy-start.6 = (f32[256,1024]{1,0:T(8,128)}, f32[256,1024]{1,0:T(8,128)S(1)}, u32[]{:S(2)}) copy-start(f32[256,1024]{1,0:T(8,128)S(1)} %fusion.84) | copy-start | bytes 3145732
  283.2 188.5 %collective-permute-start.4 = (bf16[256,2048]{0,1:T(8,128)(2,1)}, bf16[256,2048]{0,1:T(8,128)(2,1)}, u32[]{:S(2)}, u32[]{:S(2)}) collective-permute-start(bf16[256,2048]{0,1:T(8,128)(2,1)} %fusion.56), channel_id=1, source_target_pairs={{0,4},{4,0},{1,5},{5,1},{2,6},{6,2},{3,7},{7,3},{8,12},{12,8},{9,1... | collective-permute-start | bytes 3145736 | tf_op jit(solution)/shard_map/ppermute | solution.py:648
  293.7 38.1 %copy-start.24 = (bf16[256,1024]{1,0:T(8,128)(2,1)S(1)}, bf16[256,1024]{1,0:T(8,128)(2,1)}, u32[]{:S(2)}) copy-start(bf16[256,1024]{1,0:T(8,128)(2,1)} %get-tuple-element.34) | copy-start | bytes 1572868
  455.3 16.4 %copy-start.3 = (f32[16,64,512]{2,1,0:T(8,128)S(1)}, f32[16,64,512]{2,1,0:T(8,128)}, u32[]{:S(2)}) copy-start(f32[16,64,512]{2,1,0:T(8,128)} %copy-done.2) | copy-start | bytes 6291460
  455.3 16.4 %copy-start.5 = (f32[16,64,512]{2,1,0:T(8,128)S(1)}, f32[16,64,512]{2,1,0:T(8,128)}, u32[]{:S(2)}) copy-start(f32[16,64,512]{2,1,0:T(8,128)} %copy-done.4) | copy-start | bytes 6291460
  471.7 6.1 %copy-start.9 = (bf16[1024,1024]{1,0:T(8,128)(2,1)S(1)}, bf16[1024,1024]{1,0:T(8,128)(2,1)}, u32[]{:S(2)}) copy-start(bf16[1024,1024]{1,0:T(8,128)(2,1)} %key_weight.1) | copy-start | bytes 6291460
  471.7 6.1 %copy-start.17 = (f32[256,1024]{1,0:T(8,128)S(1)}, f32[256,1024]{1,0:T(8,128)}, u32[]{:S(2)}) copy-start(f32[256,1024]{1,0:T(8,128)} %fusion.179) | copy-start | bytes 3145732
  473.5 5.0 copy-start.14
  479.5 72.1 %copy-start.34 = (f32[256]{0:T(256)S(1)}, f32[256]{0:T(256)}, u32[]{:S(2)}) copy-start(f32[256]{0:T(256)} %copy-done.33) | copy-start | bytes 3076
  479.5 72.1 %copy-start.7 = (f32[256,1024]{1,0:T(8,128)S(1)}, f32[256,1024]{1,0:T(8,128)}, u32[]{:S(2)}) copy-start(f32[256,1024]{1,0:T(8,128)} %copy-done.6) | copy-start | bytes 3145732
  (17 other events, 60.1 us)
